TPU v7x, 32 devices: a whole 2x2x4 slice. The times are simulated.
32 devices in a mesh: dp: 4 (over z), wide: 8 (over y, x, core).
Axes of the slice: x: 2, y: 2, z: 4, core: 2. Of those that a mesh axis runs over, the one named last changes fastest.
Arguments:
- big_act: bfloat16 [256, 96, 729], P('dp', 'wide'), may hold values from -6 to 6
- big_cls: bfloat16 [256, 96], P('dp', 'wide'), may hold values from -6 to 6
- small_act: bfloat16 [192, 96, 121], P('dp', 'wide'), may hold values from -6 to 6
- small_cls: bfloat16 [192, 96], P('dp', 'wide'), may hold values from -6 to 6
- big_order: int32 [4, 64], P('dp'), may hold values from 0 to 63, each once within a row
- small_order: int32 [4, 48], P('dp'), may hold values from 0 to 47, each once within a row
- big_cot: bfloat16 [256, 197, 192], P(('dp', 'wide')), may hold values from -6 to 6
- small_cot: bfloat16 [192, 37, 192], P(('dp', 'wide')), may hold values from -6 to 6
- vec_params: float32 [23, 192], replicated, may hold values from -1 to 1.3
- vec_moments: float32 [2, 23, 192], replicated, as said below
- head_weight: float32 [96, 192], P('wide', 'dp'), may hold values from -0.625 to 0.625
- qkv_weight: float32 [192, 576], P('wide', 'dp'), may hold values from -0.4375 to 0.4375
- proj_weight: float32 [192, 192], P('wide', 'dp'), may hold values from -1.75 to 1.75
- up_weight: float32 [192, 768], P('wide', 'dp'), may hold values from -0.4375 to 0.4375
- down_weight: float32 [768, 192], P('wide', 'dp'), may hold values from -0.21875 to 0.21875
- head_moments: float32 [2, 96, 192], P(None, 'wide', 'dp'), as said below
- qkv_moments: float32 [2, 192, 576], P(None, 'wide', 'dp'), as said below
- proj_moments: float32 [2, 192, 192], P(None, 'wide', 'dp'), as said below
- up_moments: float32 [2, 192, 768], P(None, 'wide', 'dp'), as said below
- down_moments: float32 [2, 768, 192], P(None, 'wide', 'dp'), as said below
- basis_input: float32 [96, 96], replicated, may hold values from -1 to 1, as said below
- basis_model: float32 [6, 192, 192], replicated, may hold values from -1 to 1, as said below
- basis_qkv: float32 [576, 576], replicated, may hold values from -1 to 1, as said below
- basis_hidden: float32 [2, 768, 768], replicated, may hold values from -1 to 1, as said below
- step: int32 [1], replicated, may hold values from 2 to 20
Outputs:
- big_out: float32 [256, 197, 192], P(('dp', 'wide'))
- small_out: float32 [192, 37, 192], P(('dp', 'wide'))
- big_act_grad: float32 [256, 96, 729], P('dp', 'wide')
- big_cls_grad: float32 [256, 96], P('dp', 'wide')
- small_act_grad: float32 [192, 96, 121], P('dp', 'wide')
- small_cls_grad: float32 [192, 96], P('dp', 'wide')
- grad_norm: float32 [1], replicated
- new_vec_params: float32 [23, 192], replicated
- new_vec_moments: float32 [2, 23, 192], replicated
- new_head_weight: float32 [96, 192], P('wide', 'dp')
- new_qkv_weight: float32 [192, 576], P('wide', 'dp')
- new_proj_weight: float32 [192, 192], P('wide', 'dp')
- new_up_weight: float32 [192, 768], P('wide', 'dp')
- new_down_weight: float32 [768, 192], P('wide', 'dp')
- new_head_moments: float32 [2, 96, 192], P(None, 'wide', 'dp')
- new_qkv_moments: float32 [2, 192, 576], P(None, 'wide', 'dp')
- new_proj_moments: float32 [2, 192, 192], P(None, 'wide', 'dp')
- new_up_moments: float32 [2, 192, 768], P(None, 'wide', 'dp')
- new_down_moments: float32 [2, 768, 192], P(None, 'wide', 'dp')
- head_copy: bfloat16 [96, 192], P('wide', 'dp')
- qkv_copy: bfloat16 [192, 576], P('wide', 'dp')
- proj_copy: bfloat16 [192, 192], P('wide', 'dp')
- up_copy: bfloat16 [192, 768], P('wide', 'dp')
- down_copy: bfloat16 [768, 192], P('wide', 'dp')
Inputs may be any that keep to these rules, and one draw needn't show every extreme that they name: `big_order`: each row lists every slot index once. `small_order`: each row lists every slot index once. `vec_moments`: the roots of the second moments (index 1) are positive. `head_moments`: the roots of the second moments (index 1) are positive. `qkv_moments`: the roots of the second moments (index 1) are positive. `proj_moments`: the roots of the second moments (index 1) are positive. `up_moments`: the roots of the second moments (index 1) are positive. `down_moments`: the roots of the second moments (index 1) are positive. `basis_input`: orthogonal. `basis_model`: each member is orthogonal. `basis_qkv`: orthogonal. `basis_hidden`: each member is orthogonal.
All inputs are finite; a program needn't handle non-finite values.
Results may differ from a plain program's by a relative error of at most 0.01.
The roundings to bfloat16 on the way count: a program that leaves them out, or rounds other values in their place, can miss the bound.
Values may be sent and summed in bfloat16 or wider, within the bound.
A program may use at most 192 MiB of HBM per device.

v0:
```python
from functools import partial

import jax
import jax.numpy as jnp
import numpy as np
from jax import lax
from jax.experimental import pallas as pl
from jax.experimental.pallas import tpu as pltpu
from jax.sharding import PartitionSpec as P

HEADS = 4
HD = 48
beta_one = 0.9
beta_two = 0.999
adam_eps = 1e-08
norm_eps = 1e-06
rate_matrix = 0.08
rate_vector = 0.25
decay_rate = 0.05
clip_limit = 1.0
LANES = 256
SPLIT = 208


def nt(a, b):
    return lax.dot_general(a, b, (((1,), (1,)), ((), ())), preferred_element_type=jnp.float32)


def tn(a, b):
    return lax.dot_general(a, b, (((0,), (0,)), ((), ())), preferred_element_type=jnp.float32)


def nn(a, b):
    return jnp.dot(a, b, preferred_element_type=jnp.float32)


def colsum(v):
    return jnp.sum(v, 0, keepdims=True)


def norm_forward(rows, gain, shift):
    centered = rows - jnp.mean(rows, -1, keepdims=True)
    scale = lax.rsqrt(jnp.mean(centered * centered, -1, keepdims=True) + norm_eps)
    hat = centered * scale
    return hat, scale, (hat * gain + shift).astype(jnp.bfloat16)


def norm_backward(grad, hat, scale, gain):
    inner = grad * gain
    mean_a = jnp.mean(inner, -1, keepdims=True)
    mean_b = jnp.mean(inner * hat, -1, keepdims=True)
    return scale * (inner - mean_a - hat * mean_b)


def block_kernel(
    counts,
    tok,
    bcot,
    scot,
    vec,
    ubias,
    wh,
    wqkv,
    wp,
    wu,
    wd,
    bout,
    sout,
    gtok,
    gh,
    gqkv,
    gp,
    gu,
    gdt,
    gvec,
    gub,
    probs,
    bias,
    cot,
):
    big_n, small_n, big_len, small_len = counts
    step = pl.program_id(0)
    width = vec.shape[1]
    row_id = lax.broadcasted_iota(jnp.int32, (LANES, 1), 0)
    lane_id = lax.broadcasted_iota(jnp.int32, (1, width), 1)

    @pl.when(step == 0)
    def _():
        for ref in (gh, gqkv, gp, gu, gdt, gvec, gub):
            ref[...] = jnp.zeros_like(ref)
        cot[...] = jnp.zeros_like(cot)
        key_id = lax.broadcasted_iota(jnp.int32, (LANES, LANES), 1)
        query_id = lax.broadcasted_iota(jnp.int32, (LANES, LANES), 0)
        keep_big = (query_id < SPLIT) & (key_id < big_len)
        keep_small = (query_id >= SPLIT) & (key_id >= SPLIT) & (key_id < SPLIT + small_len)
        bias[...] = jnp.where(keep_big | keep_small, 0.0, -1e30)

    raw = jnp.transpose(tok[0].astype(jnp.float32))
    raw_low = raw.astype(jnp.bfloat16)
    is_head = (row_id == 0) | (row_id == SPLIT)
    rows = jnp.where(is_head, nn(raw_low, wh[...]) + vec[10:11], raw)
    hat_one, scale_one, normed_one = norm_forward(rows, vec[11:12], vec[12:13])
    queries = (nn(normed_one, wqkv[0]) + vec[13:14]).astype(jnp.bfloat16)
    keys_in = nn(normed_one, wqkv[1]).astype(jnp.bfloat16)
    values = (nn(normed_one, wqkv[2]) + vec[14:15]).astype(jnp.bfloat16)
    zero = jnp.zeros((), jnp.bfloat16)
    in_head = [(lane_id >= h * HD) & (lane_id < (h + 1) * HD) for h in range(HEADS)]
    mixture = jnp.zeros((LANES, width), jnp.float32)
    for h in range(HEADS):
        scores = nt(jnp.where(in_head[h], queries, zero), keys_in) * HD ** (-0.5) + bias[...]
        weights = jnp.exp(scores - jnp.max(scores, -1, keepdims=True))
        probas = weights * (1.0 / jnp.sum(weights, -1, keepdims=True))
        probs[h] = probas
        mixture += nn(probas.astype(jnp.bfloat16), jnp.where(in_head[h], values, zero))
    mixture = mixture.astype(jnp.bfloat16)
    middle = rows + nn(mixture, wp[...]) + vec[15:16]
    hat_two, scale_two, normed_two = norm_forward(middle, vec[16:17], vec[17:18])
    pre = nn(normed_two, wu[...]) + ubias[...]
    cdf = 0.5 + 0.5 * lax.erf(pre * 0.7071067811865476)
    slope = cdf + pre * jnp.exp(pre * pre * -0.5) * 0.3989422804014327
    active = (pre * cdf).astype(jnp.bfloat16)
    result = middle + nn(active, wd[...]) + vec[18:19]
    bout[0] = result[:big_len]
    cot[:big_len] = bcot[0]

    @pl.when(step < small_n)
    def _():
        sout[0] = result[SPLIT : SPLIT + small_len]
        cot[SPLIT : SPLIT + small_len] = scot[0]

    @pl.when(step == small_n)
    def _():
        cot[SPLIT:] = jnp.zeros((LANES - SPLIT, width), jnp.bfloat16)

    cot_low = cot[...]
    cot_rows = cot_low.astype(jnp.float32)
    gdt[...] += tn(cot_low, active)
    gvec[8:9] += colsum(cot_rows)
    grad_pre = (nt(cot_low, wd[...]) * slope).astype(jnp.bfloat16)
    gu[...] += tn(normed_two, grad_pre)
    gub[...] += colsum(grad_pre.astype(jnp.float32))
    grad_two = nt(grad_pre, wu[...])
    gvec[6:7] += colsum(grad_two * hat_two)
    gvec[7:8] += colsum(grad_two)
    grad_mid = norm_backward(grad_two, hat_two, scale_two, vec[16:17]) + cot_rows
    branch = grad_mid.astype(jnp.bfloat16)
    gp[...] += tn(mixture, branch)
    gvec[5:6] += colsum(branch.astype(jnp.float32))
    grad_mix = nt(branch, wp[...]).astype(jnp.bfloat16)
    grad_q = jnp.zeros((LANES, width), jnp.float32)
    grad_k = jnp.zeros((LANES, width), jnp.float32)
    grad_v = jnp.zeros((LANES, width), jnp.float32)
    for h in range(HEADS):
        probas = probs[h]
        own = jnp.where(in_head[h], grad_mix, zero)
        grad_probs = nt(own, values)
        inner = jnp.sum(probas * grad_probs, -1, keepdims=True)
        grad_scores = (probas * (grad_probs - inner)).astype(jnp.bfloat16)
        grad_q += nn(grad_scores, jnp.where(in_head[h], keys_in, zero))
        grad_k += tn(grad_scores, jnp.where(in_head[h], queries, zero))
        grad_v += tn(probas.astype(jnp.bfloat16), own)
    grad_q = (grad_q * HD ** (-0.5)).astype(jnp.bfloat16)
    grad_k = (grad_k * HD ** (-0.5)).astype(jnp.bfloat16)
    grad_v = grad_v.astype(jnp.bfloat16)
    gqkv[0] += tn(normed_one, grad_q)
    gqkv[1] += tn(normed_one, grad_k)
    gqkv[2] += tn(normed_one, grad_v)
    gvec[3:4] += colsum(grad_q.astype(jnp.float32))
    gvec[4:5] += colsum(grad_v.astype(jnp.float32))
    grad_one = nt(grad_q, wqkv[0]) + nt(grad_k, wqkv[1]) + nt(grad_v, wqkv[2])
    gvec[1:2] += colsum(grad_one * hat_one)
    gvec[2:3] += colsum(grad_one)
    grad_tok = norm_backward(grad_one, hat_one, scale_one, vec[11:12]) + grad_mid
    grad_head = jnp.where(is_head, grad_tok, 0.0).astype(jnp.bfloat16)
    gh[...] += tn(raw_low, grad_head)
    gvec[0:1] += colsum(grad_head.astype(jnp.float32))
    gtok[0] = jnp.transpose(jnp.where(is_head, nt(grad_head, wh[...]), grad_tok)).astype(jnp.bfloat16)


def whole(shape):
    return pl.BlockSpec(shape, lambda i: (0,) * len(shape))


def run_block(tok, big_cot, small_cot, vec, ubias, wh, wqkv, wp, wu, wd):
    big_n, big_len, width = big_cot.shape
    small_n, small_len = small_cot.shape[:2]
    f32 = jnp.float32
    hidden = wu.shape[1]
    outs = [
        ((big_n, big_len, width), f32),
        ((small_n, small_len, width), f32),
        (tok.shape, jnp.bfloat16),
        ((width, width), f32),
        ((3, width, width), f32),
        ((width, width), f32),
        ((width, hidden), f32),
        ((width, hidden), f32),
        ((16, width), f32),
        ((1, hidden), f32),
    ]
    one_big = pl.BlockSpec((1, big_len, width), lambda i: (i, 0, 0))
    one_small = pl.BlockSpec((1, small_len, width), lambda i: (jnp.minimum(i, small_n - 1), 0, 0))
    one_tok = pl.BlockSpec((1, width, LANES), lambda i: (i, 0, 0))
    return pl.pallas_call(
        partial(block_kernel, (big_n, small_n, big_len, small_len)),
        grid=(big_n,),
        in_specs=[one_tok, one_big, one_small]
        + [whole(a.shape) for a in (vec, ubias, wh, wqkv, wp, wu, wd)],
        out_specs=[one_big, one_small, one_tok] + [whole(s) for s, _ in outs[3:]],
        out_shape=[jax.ShapeDtypeStruct(s, d) for s, d in outs],
        scratch_shapes=[
            pltpu.VMEM((HEADS, LANES, LANES), f32),
            pltpu.VMEM((LANES, LANES), f32),
            pltpu.VMEM((LANES, width), jnp.bfloat16),
        ],
        compiler_params=pltpu.CompilerParams(vmem_limit_bytes=56 * 1024 * 1024),
        name="block",
    )(tok, big_cot, small_cot, vec, ubias, wh, wqkv, wp, wu, wd)


def row_permutation(channels, images):
    width = 192
    group = width // (2 * channels * images)
    table = np.zeros((width, width), np.float32)
    for s in range(group):
        for e in range(2):
            for c in range(channels):
                for i in range(images):
                    row = ((s * 2 + e) * channels + c) * images + i
                    table[row, i * (width // images) + s * 2 * channels + 2 * c + e] = 1.0
    return jnp.asarray(table, jnp.bfloat16)
MESH = pl.DeviceIdType.MESH
CELLS_PAD = 896
WIDTH = 192


def up_to(value, unit):
    return -(-value // unit) * unit


def spread(axis, count, me, src_of, dst, send, recv):
    copies = []
    for k in range(1, count):
        peer = lax.rem(me + k, count)
        copy = pltpu.make_async_remote_copy(
            src_ref=src_of(peer),
            dst_ref=dst,
            send_sem=send.at[k - 1],
            recv_sem=recv.at[k - 1],
            device_id={axis: peer},
            device_id_type=MESH,
        )
        copy.start()
        copies.append(copy)
    return copies


def arrived(copies):
    for copy in copies:
        copy.wait_recv()


def sent(copies):
    for copy in copies:
        copy.wait_send()


def greet(axes):
    barrier = pltpu.get_barrier_semaphore()
    total = 0
    for axis, count, me in axes:
        for k in range(1, count):
            pl.semaphore_signal(
                barrier,
                inc=1,
                device_id={axis: lax.rem(me + k, count)},
                device_id_type=MESH,
            )
        total += count - 1
    pl.semaphore_wait(barrier, total)


class Sizes:
    def __init__(self, wide, dp, channels, images, small_images):
        self.wide, self.dp = wide, dp
        self.channels, self.images, self.small_images = channels, images, small_images
        self.slots = wide * images
        self.rows = channels * self.slots
        self.piece_rows = 2 * channels * images
        self.br = WIDTH // wide
        self.bh = self.br // 2
        self.bc = WIDTH // dp
        self.pair_rows = up_to(2 * self.br, 16)
        self.block_lanes = up_to(7 * self.bc, 128)
        self.head_rows = up_to(self.bh, 16)

    def block_places(self):
        br, bh, bc = self.br, self.bh, self.bc
        return (
            [(0, 6 * bc, bh, bc)],
            [(br, 0, br, 3 * bc)],
            [(br, 3 * bc, br, bc)],
            [(0, 0, br, 4 * bc)],
            [(0, 4 * bc, br, bc), (0, 5 * bc, br, bc), (br, 4 * bc, br, bc), (br, 5 * bc, br, bc)],
        )

    def pack_blocks(self, ref, blocks):
        for block, places in zip(blocks, self.block_places()):
            at = 0
            for row, lane, rows, lanes in places:
                ref[row : row + rows, lane : lane + lanes] = block[at : at + rows]
                at += rows

    def unpack_blocks(self, packed):
        result = []
        for places in self.block_places():
            parts = [packed[r : r + n, q : q + m] for r, q, n, m in places]
            result.append(parts[0] if len(parts) == 1 else jnp.concatenate(parts, 0))
        return result


def local_columns(vec, me, sizes, member):
    channel = lax.broadcasted_iota(jnp.int32, (sizes.rows, WIDTH), 0) // sizes.slots
    lane = lax.broadcasted_iota(jnp.int32, (sizes.rows, WIDTH), 1)
    pick = (lane == 2 * (me * sizes.channels + channel) + member).astype(jnp.float32)
    return lax.dot_general(
        pick,
        vec[0:16],
        (((1,), (1,)), ((), ())),
        precision=lax.Precision.HIGHEST,
        preferred_element_type=jnp.float32,
    )


def front_kernel(
    sizes,
    lens,
    cells,
    heads,
    vec,
    table,
    perm,
    mh,
    mqkv,
    mp,
    mu,
    md,
    tok,
    wins,
    wh,
    wqkv,
    wp,
    wu,
    wd,
    stage_one,
    stage_two,
    stage_head,
    got_one,
    got_two,
    got_head,
    pooled,
    received,
    totals,
    one_send,
    one_recv,
    two_send,
    two_recv,
    head_send,
    head_recv,
    act_send,
    act_recv,
):
    bf16 = jnp.bfloat16
    me_w, me_d = lax.axis_index("wide"), lax.axis_index("dp")
    n_w, n_d = sizes.wide, sizes.dp
    br, bh, bc = sizes.br, sizes.bh, sizes.bc
    greet((("wide", n_w, me_w), ("dp", n_d, me_d)))
    stage_one[...] = jnp.zeros_like(stage_one)
    sizes.pack_blocks(stage_one, (mh[...], mqkv[...], mp[...], mu[...], md[...]))
    got_one[me_d] = stage_one[...].astype(bf16)
    one = spread("dp", n_d, me_d, lambda peer: got_one.at[me_d], got_one.at[me_d], one_send, one_recv)

    taps = [local_columns(vec, me_w, sizes, e) for e in range(2)]

    def pool(tap):
        win = nt(cells[...], table[tap * LANES : (tap + 1) * LANES, :])
        wins[tap] = win.astype(bf16)
        for e in range(2):
            part = taps[e][:, tap : tap + 1] * win
            if tap == 0:
                totals[e] = part
            else:
                totals[e] += part

    for tap in range(4):
        pool(tap)
    arrived(one)
    stage_two[...] = jnp.zeros_like(stage_two)
    stage_head[...] = jnp.zeros_like(stage_head)
    for d in range(n_d):
        head, qkv, proj, up, down = sizes.unpack_blocks(got_one[d].astype(jnp.float32))
        stage_head[0:bh, d * bc : (d + 1) * bc] = head
        stage_two[0:br, d * 4 * bc : (d + 1) * 4 * bc] = up
        for part in range(3):
            low, high = d * 3 * bc, (d + 1) * 3 * bc
            a, b = max(low, part * WIDTH), min(high, (part + 1) * WIDTH)
            if a < b:
                row = 0 if part < 2 else br
                base = (4 + part) * WIDTH if part < 2 else 0
                stage_two[row : row + br, base + a - part * WIDTH : base + b - part * WIDTH] = qkv[
                    :, a - low : b - low
                ]
        stage_two[br : 2 * br, WIDTH + d * bc : WIDTH + (d + 1) * bc] = proj
        for j in range(4):
            at = (2 + j) * WIDTH + d * bc
            stage_two[br : 2 * br, at : at + bc] = down[j * br : (j + 1) * br]
    got_two[me_w] = stage_two[...].astype(bf16)
    got_head[me_w] = stage_head[...].astype(bf16)
    two = spread("wide", n_w, me_w, lambda peer: got_two.at[me_w], got_two.at[me_w], two_send, two_recv)
    two += spread(
        "wide", n_w, me_w, lambda peer: got_head.at[me_w], got_head.at[me_w], head_send, head_recv
    )
    for tap in range(4, 9):
        pool(tap)

    big_len, small_len = lens
    lane = lax.broadcasted_iota(jnp.int32, (1, LANES), 1)
    token = ((lane >= 1) & (lane < big_len)) | ((lane > SPLIT) & (lane < SPLIT + small_len))
    for e in range(2):
        rest = jnp.zeros((), jnp.float32)
        if e == 0:
            rest = jnp.where(
                lane == 0, heads[:, 0:1], jnp.where(lane == SPLIT, heads[:, 1:2], 0.0)
            )
        full = jnp.where(token, totals[e] + taps[e][:, 9:10], rest)
        for c in range(sizes.channels):
            for w in range(n_w):
                at = (c * n_w + w) * sizes.images
                to = (e * sizes.channels + c) * sizes.images
                pooled[w, to : to + sizes.images] = full[at : at + sizes.images].astype(bf16)
    act = spread(
        "wide", n_w, me_w, lambda peer: pooled.at[peer], received.at[me_w], act_send, act_recv
    )
    received[me_w] = pooled[me_w]

    arrived(two)
    wh[...] = jnp.zeros_like(wh)
    rows_in = lax.broadcasted_iota(jnp.int32, (WIDTH, sizes.head_rows), 0)
    cols_in = lax.broadcasted_iota(jnp.int32, (WIDTH, sizes.head_rows), 1)
    heads_full = jnp.zeros((WIDTH, WIDTH), jnp.float32)
    for w in range(n_w):
        block = got_two[w]
        at = w * br
        wu[at : at + br] = block[0:br, 0 : 4 * WIDTH]
        for part in range(2):
            wqkv[part, at : at + br] = block[0:br, (4 + part) * WIDTH : (5 + part) * WIDTH]
        wqkv[2, at : at + br] = block[br : 2 * br, 0:WIDTH]
        wp[at : at + br] = block[br : 2 * br, WIDTH : 2 * WIDTH]
        for j in range(4):
            wd[4 * at + j * br : 4 * at + (j + 1) * br] = block[
                br : 2 * br, (2 + j) * WIDTH : (3 + j) * WIDTH
            ]
        place = (rows_in == 2 * (w * bh + cols_in)) & (cols_in < bh)
        heads_full += nn(place.astype(bf16), got_head[w])
    wh[...] = heads_full.astype(bf16)

    arrived(act)
    groups = n_w * sizes.piece_rows // WIDTH
    per_group = n_w // groups
    piece = WIDTH // sizes.images
    for group in range(groups):
        block = received[group * per_group : (group + 1) * per_group].reshape(WIDTH, LANES)
        moved = tn(perm[...], block)
        for image in range(sizes.images):
            tok[image, group * piece : (group + 1) * piece, :] = moved[
                image * piece : (image + 1) * piece
            ].astype(bf16)
    sent(one)
    sent(two)
    sent(act)
def tail_kernel(
    sizes,
    lens,
    gtok,
    gh,
    gqkv,
    gp,
    gu,
    gdt,
    gvec,
    gub,
    vec,
    perm,
    step,
    sh,
    sqkv,
    sp,
    su,
    sd,
    table_hbm,
    wins_hbm,
    binput_hbm,
    bmodel_hbm,
    bqkv_hbm,
    bhidden_hbm,
    dact,
    cols,
    update,
    states,
    vtotal,
    scalars,
    table,
    wins,
    binput,
    bmodel,
    bqkv,
    bhidden,
    load_sem,
    outgoing,
    returned,
    grads,
    weighted,
    tapsum,
    stage_two,
    stage_head,
    rs_send,
    rs_got,
    rsh_send,
    rsh_got,
    stage_one,
    t_send,
    t_got,
    vpart,
    v_wide,
    v_dp,
    s_wide,
    mpack,
    dirs_got,
    row_head,
    row_qkv,
    row_proj,
    row_up,
    row_down,
    y_got,
    *sems,
):
    bf16, f32 = jnp.bfloat16, jnp.float32
    me_w, me_d = lax.axis_index("wide"), lax.axis_index("dp")
    n_w, n_d = sizes.wide, sizes.dp
    br, bh, bc = sizes.br, sizes.bh, sizes.bc
    sems = iter(sems)

    def scatter(axis, src_of, dst):
        count, me = (n_w, me_w) if axis == "wide" else (n_d, me_d)
        return spread(axis, count, me, src_of, dst, next(sems), next(sems))

    loads = []
    for at, (src, dst) in enumerate(
        (
            (bmodel_hbm, bmodel),
            (bhidden_hbm, bhidden),
            (binput_hbm, binput),
            (table_hbm, table),
            (wins_hbm, wins),
            (bqkv_hbm, bqkv),
        )
    ):
        copy = pltpu.make_async_copy(src, dst, load_sem.at[at])
        copy.start()
        loads.append(copy)
    greet((("wide", n_w, me_w), ("dp", n_d, me_d)))

    groups = n_w * sizes.piece_rows // WIDTH
    per_group = n_w // groups
    piece = WIDTH // sizes.images
    for group in range(groups):
        block = jnp.concatenate(
            [
                gtok[image, group * piece : (group + 1) * piece, :].astype(f32)
                for image in range(sizes.images)
            ],
            0,
        )
        moved = nn(perm[...], block.astype(bf16)).astype(bf16)
        outgoing[group * per_group : (group + 1) * per_group] = moved.reshape(
            per_group, sizes.piece_rows, LANES
        )
    back = scatter("wide", lambda peer: outgoing.at[peer], returned.at[me_w])
    returned[me_w] = outgoing[me_w]

    for load in loads[0:3]:
        load.wait()
    even = (
        lax.broadcasted_iota(jnp.int32, (WIDTH // 2, WIDTH), 1)
        == 2 * lax.broadcasted_iota(jnp.int32, (WIDTH // 2, WIDTH), 0)
    ).astype(bf16)
    u_head = tn(binput[...].astype(bf16), nn(even, gh[...].astype(bf16)).astype(bf16))
    left = bmodel[1].astype(bf16)
    u_qkv = [tn(left, gqkv[part].astype(bf16)) for part in range(3)]
    u_proj = tn(bmodel[2].astype(bf16), gp[...].astype(bf16))
    u_up = tn(bmodel[4].astype(bf16), gu[...].astype(bf16))
    u_down = jnp.transpose(nn(gdt[...].astype(bf16), bhidden[1].astype(bf16)))
    stage_two[...] = jnp.zeros_like(stage_two)
    stage_head[...] = jnp.zeros_like(stage_head)
    for w in range(n_w):
        at = w * br
        stage_two[0:br, 0 : 4 * WIDTH] = u_up[at : at + br]
        for part in range(2):
            stage_two[0:br, (4 + part) * WIDTH : (5 + part) * WIDTH] = u_qkv[part][at : at + br]
        stage_two[br : 2 * br, 0:WIDTH] = u_qkv[2][at : at + br]
        stage_two[br : 2 * br, WIDTH : 2 * WIDTH] = u_proj[at : at + br]
        for j in range(4):
            stage_two[br : 2 * br, (2 + j) * WIDTH : (3 + j) * WIDTH] = u_down[
                4 * at + j * br : 4 * at + (j + 1) * br
            ]
        stage_head[0:bh] = u_head[w * bh : (w + 1) * bh]
        rs_send[w] = stage_two[...].astype(bf16)
        rsh_send[w] = stage_head[...].astype(bf16)
    first = scatter("wide", lambda peer: rs_send.at[peer], rs_got.at[me_w])
    first += scatter("wide", lambda peer: rsh_send.at[peer], rsh_got.at[me_w])
    rs_got[me_w] = rs_send[me_w]
    rsh_got[me_w] = rsh_send[me_w]

    mpack[...] = jnp.zeros_like(mpack)
    for half in range(2):
        sizes.pack_blocks(
            mpack.at[half], (sh[half], sqkv[half], sp[half], su[half], sd[half])
        )

    taps = [local_columns(vec, me_w, sizes, e) for e in range(2)]
    for load in loads[3:5]:
        load.wait()
    arrived(back)
    for w in range(n_w):
        block = returned[w].astype(f32)
        for e in range(2):
            for c in range(sizes.channels):
                at = (e * sizes.channels + c) * sizes.images
                to = (c * n_w + w) * sizes.images
                grads[e, to : to + sizes.images] = block[at : at + sizes.images]
    big_len, small_len = lens
    lane = lax.broadcasted_iota(jnp.int32, (1, LANES), 1)
    token = ((lane >= 1) & (lane < big_len)) | ((lane > SPLIT) & (lane < SPLIT + small_len))
    lane_low = lax.broadcasted_iota(jnp.int32, (1, 128), 1)
    half_rows = sizes.channels * 8

    def collect(product):
        part = jnp.sum(product.reshape(sizes.channels, sizes.slots // 8, 8, LANES), 1)
        return jnp.sum(part.reshape(half_rows, LANES), -1, keepdims=True)

    for e in range(2):
        tapsum[e] = jnp.where(lane_low == 9, collect(jnp.where(token, grads[e], 0.0)), 0.0)
    for tap in range(9):
        win = wins[tap].astype(f32)
        mixed = jnp.zeros((), f32)
        for e in range(2):
            tapsum[e] = jnp.where(lane_low == tap, collect(grads[e] * win), tapsum[e])
            mixed += taps[e][:, tap : tap + 1] * grads[e]
        weighted[:, tap * LANES : (tap + 1) * LANES] = mixed.astype(bf16)
    cols[...] = jnp.where(lane_low == 0, grads[0, :, 0:128], grads[0, :, 128:256])

    @pl.loop(0, sizes.rows // 256)
    def _(chunk):
        at = pl.ds(pl.multiple_of(chunk * 256, 256), 256)
        dact[at, :] = nn(weighted[at, :], table[...])

    vpart[...] = jnp.zeros_like(vpart)
    own_channel = lax.broadcasted_iota(jnp.int32, (half_rows, WIDTH), 0) // 8
    own_lane = lax.broadcasted_iota(jnp.int32, (half_rows, WIDTH), 1)
    conv = jnp.zeros((128, WIDTH), f32)
    for e in range(2):
        place = (own_lane == 2 * (me_w * sizes.channels + own_channel) + e).astype(f32)
        conv += lax.dot_general(
            tapsum[e],
            place,
            (((0,), (0,)), ((), ())),
            precision=lax.Precision.HIGHEST,
            preferred_element_type=f32,
        )
    vpart[0:10] = conv[0:10]
    vpart[10:19] = gvec[0:9]
    for j in range(4):
        vpart[19 + j : 20 + j] = gub[:, j * WIDTH : (j + 1) * WIDTH]
    v_wide[me_w] = vpart[...]
    vec_one = scatter("wide", lambda peer: v_wide.at[me_w], v_wide.at[me_w])

    loads[5].wait()
    arrived(first)
    rows_two = rs_got[0].astype(f32)
    rows_head = rsh_got[0].astype(f32)
    for w in range(1, n_w):
        rows_two += rs_got[w].astype(f32)
        rows_head += rsh_got[w].astype(f32)
    rows_two = rows_two.astype(bf16)
    right = bqkv[...].astype(bf16)
    t_up = nn(rows_two[0:br, 0 : 4 * WIDTH], bhidden[0].astype(bf16))
    t_qkv = nn(rows_two[0:br, 4 * WIDTH : 6 * WIDTH], right[0 : 2 * WIDTH]) + nn(
        rows_two[br : 2 * br, 0:WIDTH], right[2 * WIDTH :]
    )
    t_proj = nn(rows_two[br : 2 * br, WIDTH : 2 * WIDTH], bmodel[3].astype(bf16))
    right = bmodel[5].astype(bf16)
    t_down = [
        nn(rows_two[br : 2 * br, (2 + j) * WIDTH : (3 + j) * WIDTH], right) for j in range(4)
    ]
    t_head = nn(rows_head.astype(bf16), bmodel[0].astype(bf16))
    stage_one[...] = jnp.zeros_like(stage_one)
    for d in range(n_d):
        own = slice(d * bc, (d + 1) * bc)
        sizes.pack_blocks(
            stage_one,
            (
                t_head[0:bh, own],
                t_qkv[:, 3 * d * bc : 3 * (d + 1) * bc],
                t_proj[:, own],
                t_up[:, 4 * d * bc : 4 * (d + 1) * bc],
                jnp.concatenate([t[:, own] for t in t_down], 0),
            ),
        )
        t_send[d] = stage_one[...].astype(bf16)
    second = scatter("dp", lambda peer: t_send.at[peer], t_got.at[me_d])
    t_got[me_d] = t_send[me_d]

    arrived(vec_one)
    vsum = v_wide[0]
    for w in range(1, n_w):
        vsum += v_wide[w]
    arrived(second)
    turned = t_got[0].astype(f32)
    for d in range(1, n_d):
        turned += t_got[d].astype(f32)
    own_square = jnp.sum(jnp.sum(turned * turned, -1, keepdims=True), 0, keepdims=True)
    last_row = lax.broadcasted_iota(jnp.int32, vsum.shape, 0) == vsum.shape[0] - 1
    v_dp[me_d] = jnp.where(last_row, own_square, vsum)
    vec_two = scatter("dp", lambda peer: v_dp.at[me_d], v_dp.at[me_d])
    arrived(vec_two)
    vsum = v_dp[0]
    for d in range(1, n_d):
        vsum += v_dp[d]
    s_wide[me_w] = jnp.broadcast_to(vsum[23:24, 0:128], (8, 128))
    third = scatter("wide", lambda peer: s_wide.at[me_w], s_wide.at[me_w])
    vsum = jnp.where(last_row, 0.0, vsum)
    vtotal[...] = vsum
    vec_square = jnp.sum(jnp.sum(vsum * vsum, -1, keepdims=True), 0, keepdims=True)
    count = jnp.full((8, 128), step[0], jnp.int32).astype(f32)[0:1, 0:1]
    fix_one = 1.0 - jnp.exp(count * float(np.log(beta_one)))
    fix_two = 1.0 - jnp.exp(count * float(np.log(beta_two)))
    arrived(third)
    square = s_wide[0][0:1, 0:1]
    for w in range(1, n_w):
        square += s_wide[w][0:1, 0:1]
    norm = jnp.sqrt(square + vec_square)
    factor = jnp.minimum(1.0, clip_limit / (norm + 1e-06))
    which = lax.broadcasted_iota(jnp.int32, (8, 128), 1)
    scalars[...] = jnp.where(
        which == 0,
        norm,
        jnp.where(which == 1, factor, jnp.where(which == 2, fix_one, fix_two)),
    )

    turned = turned * factor
    moment = beta_one * mpack[0] + (1.0 - beta_one) * turned
    second_moment = beta_two * mpack[1] * mpack[1] + (1.0 - beta_two) * turned * turned
    states[0] = moment
    states[1] = jnp.sqrt(second_moment)
    direction = moment / fix_one / (jnp.sqrt(second_moment / fix_two) + adam_eps)
    dirs_got[me_d] = direction.astype(bf16)
    fourth = scatter("dp", lambda peer: dirs_got.at[me_d], dirs_got.at[me_d])
    arrived(fourth)
    for d in range(n_d):
        head, qkv, proj, up, down = sizes.unpack_blocks(dirs_got[d].astype(f32))
        row_head[0:bh, d * bc : (d + 1) * bc] = head
        row_qkv[:, 3 * d * bc : 3 * (d + 1) * bc] = qkv
        row_proj[:, d * bc : (d + 1) * bc] = proj
        row_up[:, 4 * d * bc : 4 * (d + 1) * bc] = up
        row_down[:, d * bc : (d + 1) * bc] = down

    def right_rows(ref, size):
        return ref[pl.ds(pl.multiple_of(me_d * size, 8), size), :].astype(bf16)

    stage_one[...] = jnp.zeros_like(stage_one)
    sizes.pack_blocks(
        stage_one,
        (
            nt(row_head[...].astype(bf16), right_rows(bmodel.at[0], bc))[0:bh],
            nt(row_qkv[...].astype(bf16), right_rows(bqkv, 3 * bc)),
            nt(row_proj[...].astype(bf16), right_rows(bmodel.at[3], bc)),
            nt(row_up[...].astype(bf16), right_rows(bhidden.at[0], 4 * bc)),
            nt(row_down[...].astype(bf16), right_rows(bmodel.at[5], bc)),
        ),
    )
    y_got[me_w] = stage_one[...].astype(bf16)
    fifth = scatter("wide", lambda peer: y_got.at[me_w], y_got.at[me_w])
    def left_rows(ref, size):
        if size % 8 == 0:
            return ref[pl.ds(pl.multiple_of(me_w * size, 8), size), :].astype(bf16)
        own = lax.broadcasted_iota(jnp.int32, (size, ref.shape[0]), 0) + me_w * size
        pick = own == lax.broadcasted_iota(jnp.int32, (size, ref.shape[0]), 1)
        return nn(pick.astype(bf16), ref[...].astype(bf16)).astype(bf16)

    lefts = (
        left_rows(binput, bh),
        left_rows(bmodel.at[1], br),
        left_rows(bmodel.at[2], br),
        left_rows(bmodel.at[4], br),
        left_rows(bhidden.at[1], 4 * br),
    )
    arrived(fifth)
    parts = [sizes.unpack_blocks(y_got[w].astype(f32)) for w in range(n_w)]
    update[...] = jnp.zeros_like(update)
    sizes.pack_blocks(
        update,
        [
            nn(
                lefts[member],
                jnp.concatenate([part[member] for part in parts], 0).astype(bf16),
            )
            for member in range(5)
        ],
    )
    for copies in (back, first, vec_one, second, vec_two, third, fourth, fifth):
        sent(copies)


def finish_kernel(
    sizes, mh, mqkv, mp, mu, md, vec, vmom, update, states, vtotal, scalars, nvec, nvmom, *outs
):
    factor, fix_one, fix_two = (scalars[0:1, j : j + 1] for j in (1, 2, 3))
    updates = sizes.unpack_blocks(update[...])
    firsts = sizes.unpack_blocks(states[0])
    seconds = sizes.unpack_blocks(states[1])
    for member, master in enumerate((mh, mqkv, mp, mu, md)):
        fresh = master[...] - rate_matrix * updates[member]
        outs[member][...] = fresh
        outs[5 + member][0] = firsts[member]
        outs[5 + member][1] = seconds[member]
        outs[10 + member][...] = fresh.astype(jnp.bfloat16)
    scaled = vtotal[0:23] * factor
    first = beta_one * vmom[0] + (1.0 - beta_one) * scaled
    second = beta_two * vmom[1] * vmom[1] + (1.0 - beta_two) * scaled * scaled
    direction = first / fix_one / (jnp.sqrt(second / fix_two) + adam_eps)
    nvec[...] = vec[...] * (1.0 - rate_vector * decay_rate) - rate_vector * direction
    nvmom[0] = first
    nvmom[1] = jnp.sqrt(second)


VM = pl.BlockSpec(memory_space=pltpu.VMEM)
SM = pl.BlockSpec(memory_space=pltpu.SMEM)
HB = pl.BlockSpec(memory_space=pl.ANY)
LIMIT = 60 * 1024 * 1024


def dma_sems(*counts):
    return [pltpu.SemaphoreType.DMA((n,)) for n in counts]


def run_front(sizes, lens, cells, heads, vec, table, perm, masters):
    bf16, f32 = jnp.bfloat16, jnp.float32
    w, d = sizes.wide, sizes.dp
    outs = [
        ((sizes.images, WIDTH, LANES), bf16),
        ((9, sizes.rows, LANES), bf16),
        ((WIDTH, WIDTH), bf16),
        ((3, WIDTH, WIDTH), bf16),
        ((WIDTH, WIDTH), bf16),
        ((WIDTH, 4 * WIDTH), bf16),
        ((4 * WIDTH, WIDTH), bf16),
    ]
    return pl.pallas_call(
        partial(front_kernel, sizes, lens),
        in_specs=[VM] * 10,
        out_specs=[VM] * len(outs),
        out_shape=[jax.ShapeDtypeStruct(s, t) for s, t in outs],
        scratch_shapes=[
            pltpu.VMEM((sizes.pair_rows, sizes.block_lanes), f32),
            pltpu.VMEM((sizes.pair_rows, 6 * WIDTH), f32),
            pltpu.VMEM((sizes.head_rows, WIDTH), f32),
            pltpu.VMEM((d, sizes.pair_rows, sizes.block_lanes), bf16),
            pltpu.VMEM((w, sizes.pair_rows, 6 * WIDTH), bf16),
            pltpu.VMEM((w, sizes.head_rows, WIDTH), bf16),
            pltpu.VMEM((w, sizes.piece_rows, LANES), bf16),
            pltpu.VMEM((w, sizes.piece_rows, LANES), bf16),
            pltpu.VMEM((2, sizes.rows, LANES), f32),
        ]
        + dma_sems(d - 1, d - 1, w - 1, w - 1, w - 1, w - 1, w - 1, w - 1),
        compiler_params=pltpu.CompilerParams(
            collective_id=0, has_side_effects=True, vmem_limit_bytes=LIMIT
        ),
        name="front",
    )(cells, heads, vec, table, perm, *masters)


def run_tail(sizes, lens, grads, vec, perm, step, moments, table, wins, bases):
    bf16, f32 = jnp.bfloat16, jnp.float32
    w, d = sizes.wide, sizes.dp
    pack = (sizes.pair_rows, sizes.block_lanes)
    outs = [
        ((sizes.rows, CELLS_PAD), f32),
        ((sizes.rows, 128), f32),
        (pack, f32),
        ((2,) + pack, f32),
        ((24, WIDTH), f32),
        ((8, 128), f32),
    ]
    two = (sizes.pair_rows, 6 * WIDTH)
    head = (sizes.head_rows, WIDTH)
    piece = (w, sizes.piece_rows, LANES)
    return pl.pallas_call(
        partial(tail_kernel, sizes, lens),
        in_specs=[VM] * 10 + [SM] + [VM] * 5 + [HB] * 6,
        out_specs=[VM] * len(outs),
        out_shape=[jax.ShapeDtypeStruct(s, t) for s, t in outs],
        scratch_shapes=[pltpu.VMEM(a.shape, a.dtype) for a in (table, wins, *bases)]
        + dma_sems(6)
        + [
            pltpu.VMEM(piece, bf16),
            pltpu.VMEM(piece, bf16),
            pltpu.VMEM((2, sizes.rows, LANES), f32),
            pltpu.VMEM((sizes.rows, 9 * LANES), bf16),
            pltpu.VMEM((2, sizes.channels * 8, 128), f32),
            pltpu.VMEM(two, f32),
            pltpu.VMEM(head, f32),
            pltpu.VMEM((w,) + two, bf16),
            pltpu.VMEM((w,) + two, bf16),
            pltpu.VMEM((w,) + head, bf16),
            pltpu.VMEM((w,) + head, bf16),
            pltpu.VMEM(pack, f32),
            pltpu.VMEM((d,) + pack, bf16),
            pltpu.VMEM((d,) + pack, bf16),
            pltpu.VMEM((24, WIDTH), f32),
            pltpu.VMEM((w, 24, WIDTH), f32),
            pltpu.VMEM((d, 24, WIDTH), f32),
            pltpu.VMEM((w, 8, 128), f32),
            pltpu.VMEM((2,) + pack, f32),
            pltpu.VMEM((d,) + pack, bf16),
            pltpu.VMEM((sizes.bh, WIDTH), f32),
            pltpu.VMEM((sizes.br, 3 * WIDTH), f32),
            pltpu.VMEM((sizes.br, WIDTH), f32),
            pltpu.VMEM((sizes.br, 4 * WIDTH), f32),
            pltpu.VMEM((4 * sizes.br, WIDTH), f32),
            pltpu.VMEM((w,) + pack, bf16),
        ]
        + dma_sems(
            *(n - 1 for n in (w, w, w, w, w, w, w, w, d, d, d, d, w, w, d, d, w, w))
        ),
        compiler_params=pltpu.CompilerParams(
            collective_id=1, has_side_effects=True, vmem_limit_bytes=LIMIT
        ),
        name="tail",
    )(*grads, vec, perm, step, *moments, table, wins, *bases)


def run_finish(sizes, masters, vec, vmom, packs):
    f32, bf16 = jnp.float32, jnp.bfloat16
    shapes = [m.shape for m in masters]
    outs = [(vec.shape, f32), (vmom.shape, f32)]
    outs += [(s, f32) for s in shapes] + [((2,) + s, f32) for s in shapes]
    outs += [(s, bf16) for s in shapes]
    return pl.pallas_call(
        partial(finish_kernel, sizes),
        in_specs=[VM] * 11,
        out_specs=[VM] * len(outs),
        out_shape=[jax.ShapeDtypeStruct(s, t) for s, t in outs],
        name="finish",
    )(*masters, vec, vmom, *packs)


def pool_table(grids):
    table = np.zeros((9, LANES, CELLS_PAD), np.float32)
    base = 0
    for grid, side, lane in grids:
        for tap in range(9):
            for y in range(side):
                for x in range(side):
                    sy, sx = 2 * y + tap // 3 - 1, 2 * x + tap % 3 - 1
                    if 0 <= sy < grid and 0 <= sx < grid:
                        table[tap, lane + y * side + x, base + sy * grid + sx] = 1.0
        base += grid * grid
    return jnp.asarray(table.reshape(9 * LANES, CELLS_PAD), jnp.bfloat16)


def per_device(
    wide_n,
    dp_n,
    big_act,
    big_cls,
    small_act,
    small_cls,
    big_order,
    small_order,
    big_cot,
    small_cot,
    vec_params,
    vec_moments,
    *rest,
):
    masters, moments, bases, step = rest[0:5], rest[5:10], rest[10:14], rest[14]
    channels = big_act.shape[1]
    images, small_images = big_cot.shape[0], small_cot.shape[0]
    lens = (big_cot.shape[1], small_cot.shape[1])
    sizes = Sizes(wide_n, dp_n, channels, images, small_images)
    big_cells, small_cells = big_act.shape[2], small_act.shape[2]
    grids = tuple(
        (int(cells**0.5), int((length - 1) ** 0.5), lane)
        for cells, length, lane in ((big_cells, lens[0], 1), (small_cells, lens[1], SPLIT + 1))
    )
    table = pool_table(grids)
    perm = row_permutation(channels, images)
    take = lambda a, i, axis: jnp.take(a, i, axis=axis, mode="clip")

    big_slots = big_order[0]
    small_slots = jnp.pad(
        small_order[0].reshape(wide_n, small_images), ((0, 0), (0, images - small_images))
    ).reshape(-1)
    cells = jnp.concatenate(
        [
            take(big_act, big_slots, 0),
            take(small_act, small_slots, 0),
            jnp.zeros(
                (big_slots.shape[0], channels, CELLS_PAD - big_cells - small_cells), jnp.bfloat16
            ),
        ],
        2,
    )
    cells = jnp.swapaxes(cells, 0, 1).reshape(sizes.rows, CELLS_PAD)
    heads = jnp.stack([take(big_cls, big_slots, 0), take(small_cls, small_slots, 0)], 2)
    heads = jnp.swapaxes(heads, 0, 1).reshape(sizes.rows, 2).astype(jnp.float32)

    tok, wins, wh, wqkv, wp, wu, wd = run_front(
        sizes, lens, cells, heads, vec_params, table, perm, masters
    )
    hidden = wu.shape[1]
    block = run_block(
        tok, big_cot, small_cot, vec_params, vec_params[19:].reshape(1, hidden), wh, wqkv, wp, wu, wd
    )
    dact, cols, update, states, vtotal, scalars = run_tail(
        sizes, lens, block[2:], vec_params, perm, step, moments, table, wins, bases
    )
    results = run_finish(
        sizes, masters, vec_params, vec_moments, (update, states, vtotal, scalars)
    )

    ids = lambda n: jnp.arange(n, dtype=jnp.int32)
    big_count, small_count = big_act.shape[0], small_act.shape[0]
    big_inverse = jnp.sum(
        jnp.where(big_slots[:, None] == ids(big_count)[None], ids(big_count)[:, None], 0), 0
    )
    small_at = ids(small_count) // small_images * images + ids(small_count) % small_images
    small_inverse = jnp.sum(
        jnp.where(small_order[0][:, None] == ids(small_count)[None], small_at[:, None], 0), 0
    )
    dact = dact.reshape(channels, sizes.slots, CELLS_PAD)
    cols = cols.reshape(channels, sizes.slots, 128)
    low = SPLIT - 128
    big_act_grad = jnp.swapaxes(take(dact[:, :, :big_cells], big_inverse, 1), 0, 1)
    small_act_grad = jnp.swapaxes(
        take(dact[:, :, big_cells : big_cells + small_cells], small_inverse, 1), 0, 1
    )
    big_cls_grad = jnp.swapaxes(take(cols[:, :, 0], big_inverse, 1), 0, 1)
    small_cls_grad = jnp.swapaxes(take(cols[:, :, low], small_inverse, 1), 0, 1)
    return (
        block[0],
        block[1],
        big_act_grad,
        big_cls_grad,
        small_act_grad,
        small_cls_grad,
        scalars[0, 0:1],
        *results,
    )


def solution(mesh):
    split, wide_first, free = P("dp", "wide", None), P("wide", "dp"), P()
    moment = P(None, "wide", "dp")
    both = P(("dp", "wide"), None, None)
    acts = (split, P("dp", "wide"), split, P("dp", "wide"))
    in_specs = (
        acts
        + (P("dp", None), P("dp", None), both, both, free, free)
        + (wide_first,) * 5
        + (moment,) * 5
        + (free,) * 5
    )
    out_specs = (
        (both, both) + acts + (free,) * 3 + (wide_first,) * 5 + (moment,) * 5 + (wide_first,) * 5
    )
    return jax.shard_map(
        partial(per_device, mesh.shape["wide"], mesh.shape["dp"]),
        mesh=mesh,
        in_specs=in_specs,
        out_specs=out_specs,
        check_vma=False,
    )
```

profile of v0, /device:TPU:1, one launch (start us, length us, event | category | flops | bytes accessed | tf_op | source)
XLA Modules:
  0.0 186.8 jit_solution(15498232855489287252)
XLA Ops:
  1.2 1.3 reduce.3
  2.7 2.2 %gather_fusion.1 = bf16[64,12,121]{2,0,1:T(8,128)(2,1)S(1)} fusion(bf16[48,12,121]{2,0,1:T(8,128)(2,1)} %param.29, s32[1024]{0:T(1024)S(1)} %pad_clamp_fusion.2), kind=kCustom, calls=%fused_computation.1 | custom fusion | bytes 371968 | tf_op jit(solution)/shard_map/jit(_take)/gather | solution.py:1008
  4.9 4.0 %gather_fusion = bf16[64,12,729]{2,0,1:T(8,128)(2,1)S(1)} fusion(bf16[64,12,729]{2,0,1:T(8,128)(2,1)S(1)} %copy-done, s32[1024]{0:T(1024)S(1)} %pad_clamp_fusion.3), kind=kCustom, calls=%fused_computation | custom fusion | bytes 2239744 | tf_op jit(solution)/shard_map/jit(_take)/gather | solution.py:1008
  9.1 1.5 maximum_maximum_fusion
  12.3 1.0 copy.122
  13.9 35.0 %front.1 = (bf16[8,192,256]{2,1,0:T(8,128)(2,1)}, bf16[9,768,256]{2,1,0:T(8,128)(2,1)}, bf16[192,192]{1,0:T(8,128)(2,1)}, bf16[3,192,192]{2,1,0:T(8,128)(2,1)}, ...) custom-call(bf16[768,896]{1,0:T(8,128)(2,1)} %bitcast.15, f32[768,2]{1,0:T(8,128)} %bitcast.19, ...), custom_call_target="tpu_custom_call" | custom-call | tf_op jit(solution)/shard_map/front/pallas_call | solution.py:868
  49.0 1.3 copy.124.bcot
  51.6 47.3 %block.1 = (f32[8,197,192]{2,1,0:T(8,128)}, f32[6,37,192]{2,1,0:T(8,128)}, bf16[8,192,256]{2,1,0:T(8,128)(2,1)}, f32[192,192]{1,0:T(8,128)}, f32[3,192,192]{2,1,...) custom-call(bf16[8,192,256]{2,1,0:T(8,128)(2,1)} %get-tuple-element., ...), custom_call_target="tpu_custom_call" | custom-call | tf_op jit(solution)/shard_map/block/pallas_call | solution.py:204
  98.9 2.7 %copy.133 = f32[8,197,192]{1,2,0:T(8,128)} copy(f32[8,197,192]{2,1,0:T(8,128)} %get-tuple-element.176) | data formatting | bytes 2420736
  102.9 0.7 copy.126.sd
  103.6 51.2 %tail.1 = (f32[768,896]{1,0:T(8,128)}, f32[768,128]{1,0:T(8,128)}, f32[48,384]{1,0:T(8,128)}, f32[2,48,384]{2,1,0:T(8,128)}, f32[24,192]{1,0:T(8,128)}, /*index=5*/f32[8,128]{1,0:T(8,128)}) custom-call(bf16[8,192,256]{2,1,0:T(8,128)(2,1)} %get-tuple-element.72.gtok, f32[192,192]{1,0:T(8,128)} %get-tuple-element.73.gh, ...), custom_call_target="tpu_custom_call" | custom-call | tf_op jit(solution)/shard_map/tail/pallas_call | solution.py:907
  154.8 1.9 %slice.40 = f32[12,64,729]{2,1,0:T(8,128)S(1)} slice(f32[12,64,896]{2,1,0:T(8,128)} %bitcast.16), slice={[0:12], [0:64], [0:729]} | slice | bytes 4478976 | tf_op jit(solution)/shard_map/slice | solution.py:1054
  156.7 3.0 %copy.143 = f32[12,64,729]{2,0,1:T(8,128)} copy(f32[12,64,729]{2,1,0:T(8,128)S(1)} %slice.40) | data formatting | bytes 4478976
  159.9 4.3 %gather_fusion.4 = f32[64,12,729]{2,1,0:T(8,128)} fusion(f32[12,64,729]{2,0,1:T(8,128)} %copy.143, s32[1024]{0:T(1024)S(1)} %pad_clamp_fusion.1), kind=kCustom, calls=%fused_computation.4 | custom fusion | bytes 4479232 | tf_op jit(solution)/shard_map/jit(_take)/gather | solution.py:1008
  164.2 4.7 %copy.134 = f32[64,12,729]{2,0,1:T(8,128)} copy(f32[64,12,729]{2,1,0:T(8,128)} %gather_fusion.4) | data formatting | bytes 4478976
  170.9 1.3 slice.42
  173.2 0.8 copy.136
  175.7 1.2 slice.23
  177.5 2.0 %finish.1 = (f32[23,192]{1,0:T(8,128)}, f32[2,23,192]{2,1,0:T(8,128)}, f32[12,48]{1,0:T(8,128)}, f32[24,144]{1,0:T(8,128)}, f32[24,48]{1,0:T(8,128)}, /*index=5*...) custom-call(f32[12,48]{1,0:T(8,128)} %mh.3, ...), custom_call_target="tpu_custom_call" | custom-call | tf_op jit(solution)/shard_map/finish/pallas_call | solution.py:958
  179.5 1.4 copy.138
  181.0 1.5 copy.139
  182.4 1.3 copy.140
  183.8 1.6 copy.141
  185.4 1.4 copy.142
  (56 shorter events, 10.6 us)
Async XLA Ops:
  0.7 4.3 %copy-start = (bf16[64,12,729]{2,0,1:T(8,128)(2,1)S(1)}, bf16[64,12,729]{2,0,1:T(8,128)(2,1)}, u32[]{:S(2)}) copy-start(bf16[64,12,729]{2,0,1:T(8,128)(2,1)} %param.27) | copy-start | bytes 3359236
  0.7 4.2 %copy-start.9 = (s32[1,64]{1,0:T(1,128)S(1)}, s32[1,64]{1,0:T(1,128)}, u32[]{:S(2)}) copy-start(s32[1,64]{1,0:T(1,128)} %param.31) | copy-start | bytes 772
  8.9 1.6 copy-start.8
  9.0 2.4 %copy-start.7 = (bf16[64,12]{0,1:T(8,128)(2,1)S(1)}, bf16[64,12]{0,1:T(8,128)(2,1)}, u32[]{:S(2)}) copy-start(bf16[64,12]{0,1:T(8,128)(2,1)} %param.28) | copy-start | bytes 4612
  9.0 4.3 %copy-start.5 = (f32[96,48]{0,1:T(8,128)S(1)}, f32[96,48]{0,1:T(8,128)}, u32[]{:S(2)}) copy-start(f32[96,48]{0,1:T(8,128)} %param.41) | copy-start | bytes 55300
  13.9 35.0 %copy-start.2 = (bf16[8,197,192]{1,2,0:T(8,128)(2,1)S(1)}, bf16[8,197,192]{1,2,0:T(8,128)(2,1)}, u32[]{:S(2)}) copy-start(bf16[8,197,192]{1,2,0:T(8,128)(2,1)} %param.33) | copy-start | bytes 1815556
  51.6 50.7 %copy-start.6 = (f32[2,12,48]{2,0,1:T(2,128)S(1)}, f32[2,12,48]{2,0,1:T(2,128)}, u32[]{:S(2)}) copy-start(f32[2,12,48]{2,0,1:T(2,128)} %param.42) | copy-start | bytes 13828
  98.9 4.0 %copy-start.3 = (f32[2,96,48]{1,2,0:T(8,128)S(1)}, f32[2,96,48]{1,2,0:T(8,128)}, u32[]{:S(2)}) copy-start(f32[2,96,48]{1,2,0:T(8,128)} %param.46) | copy-start | bytes 110596
  164.2 4.7 %copy-start.1 = (f32[768,128]{1,0:T(8,128)S(1)}, f32[768,128]{1,0:T(8,128)}, u32[]{:S(2)}) copy-start(f32[768,128]{1,0:T(8,128)} %get-tuple-element.82) | copy-start | bytes 1179652
  168.9 3.5 %copy-start.10 = (s32[1,48]{1,0:T(1,128)S(1)}, s32[1,48]{1,0:T(1,128)}, u32[]{:S(2)}) copy-start(s32[1,48]{1,0:T(1,128)} %param.32) | copy-start | bytes 580
  169.1 7.8 %copy-start.4 = (f32[2,23,192]{2,0,1:T(2,128)S(1)}, f32[2,23,192]{2,0,1:T(2,128)}, u32[]{:S(2)}) copy-start(f32[2,23,192]{2,0,1:T(2,128)} %param.36) | copy-start | bytes 105988
where the time goes:
time: 188 us; the launch traced here: 187 us
  Pallas kernels  135 us (72%)
  local copies, waits for them, and re-layouts  46.7 us (25%)
  other arithmetic  3.05 us (2%)
    pallas_call x1, Pallas kernels, run_tail(): pl.pallas_call(partial(tail_kernel, sizes, lens), in_specs=[VM] * 10 + [S...  51.2 us
    pallas_call x1, Pallas kernels, run_block(): pl.pallas_call(partial(block_kernel, (big_n, small_n, big_len, small_len)...  47.3 us
    pallas_call x1, Pallas kernels, run_front(): pl.pallas_call(partial(front_kernel, sizes, lens), in_specs=[VM] * 10, ou...  35 us
    unnamed x44, local copies, waits for them, and re-layouts  25.8 us
    gather x8, local copies, waits for them, and re-layouts, per_device(): take = lambda a, i, axis: jnp.take(a, i, axis=axis, mode='clip')  13.6 us

commit v1 on v0

--- a/solution.py
+++ b/solution.py
@@ -58,7 +58,6 @@
     bcot,
     scot,
     vec,
-    ubias,
     wh,
     wqkv,
     wp,
@@ -77,6 +76,7 @@
     probs,
     bias,
     cot,
+    ubias,
 ):
     big_n, small_n, big_len, small_len = counts
     step = pl.program_id(0)
@@ -89,6 +89,8 @@
         for ref in (gh, gqkv, gp, gu, gdt, gvec, gub):
             ref[...] = jnp.zeros_like(ref)
         cot[...] = jnp.zeros_like(cot)
+        for j in range(4):
+            ubias[:, j * width : (j + 1) * width] = vec[19 + j : 20 + j]
         key_id = lax.broadcasted_iota(jnp.int32, (LANES, LANES), 1)
         query_id = lax.broadcasted_iota(jnp.int32, (LANES, LANES), 0)
         keep_big = (query_id < SPLIT) & (key_id < big_len)
@@ -120,8 +122,8 @@
     slope = cdf + pre * jnp.exp(pre * pre * -0.5) * 0.3989422804014327
     active = (pre * cdf).astype(jnp.bfloat16)
     result = middle + nn(active, wd[...]) + vec[18:19]
-    bout[0] = result[:big_len]
-    cot[:big_len] = bcot[0]
+    bout[0] = jnp.transpose(result)[:, :big_len]
+    cot[:big_len] = jnp.transpose(bcot[0].astype(jnp.float32)).astype(jnp.bfloat16)
 
     @pl.when(step < small_n)
     def _():
@@ -181,13 +183,13 @@
     return pl.BlockSpec(shape, lambda i: (0,) * len(shape))
 
 
-def run_block(tok, big_cot, small_cot, vec, ubias, wh, wqkv, wp, wu, wd):
-    big_n, big_len, width = big_cot.shape
+def run_block(tok, big_cot, small_cot, vec, wh, wqkv, wp, wu, wd):
+    big_n, width, big_len = big_cot.shape
     small_n, small_len = small_cot.shape[:2]
     f32 = jnp.float32
     hidden = wu.shape[1]
     outs = [
-        ((big_n, big_len, width), f32),
+        ((big_n, width, big_len), f32),
         ((small_n, small_len, width), f32),
         (tok.shape, jnp.bfloat16),
         ((width, width), f32),
@@ -198,24 +200,25 @@
         ((16, width), f32),
         ((1, hidden), f32),
     ]
-    one_big = pl.BlockSpec((1, big_len, width), lambda i: (i, 0, 0))
+    one_big = pl.BlockSpec((1, width, big_len), lambda i: (i, 0, 0))
     one_small = pl.BlockSpec((1, small_len, width), lambda i: (jnp.minimum(i, small_n - 1), 0, 0))
     one_tok = pl.BlockSpec((1, width, LANES), lambda i: (i, 0, 0))
     return pl.pallas_call(
         partial(block_kernel, (big_n, small_n, big_len, small_len)),
         grid=(big_n,),
         in_specs=[one_tok, one_big, one_small]
-        + [whole(a.shape) for a in (vec, ubias, wh, wqkv, wp, wu, wd)],
+        + [whole(a.shape) for a in (vec, wh, wqkv, wp, wu, wd)],
         out_specs=[one_big, one_small, one_tok] + [whole(s) for s, _ in outs[3:]],
         out_shape=[jax.ShapeDtypeStruct(s, d) for s, d in outs],
         scratch_shapes=[
             pltpu.VMEM((HEADS, LANES, LANES), f32),
             pltpu.VMEM((LANES, LANES), f32),
             pltpu.VMEM((LANES, width), jnp.bfloat16),
+            pltpu.VMEM((1, hidden), f32),
         ],
         compiler_params=pltpu.CompilerParams(vmem_limit_bytes=56 * 1024 * 1024),
         name="block",
-    )(tok, big_cot, small_cot, vec, ubias, wh, wqkv, wp, wu, wd)
+    )(tok, big_cot, small_cot, vec, wh, wqkv, wp, wu, wd)
 
 
 def row_permutation(channels, images):
@@ -230,7 +233,6 @@
                     table[row, i * (width // images) + s * 2 * channels + 2 * c + e] = 1.0
     return jnp.asarray(table, jnp.bfloat16)
 MESH = pl.DeviceIdType.MESH
-CELLS_PAD = 896
 WIDTH = 192
 
 
@@ -286,6 +288,8 @@
         self.channels, self.images, self.small_images = channels, images, small_images
         self.slots = wide * images
         self.rows = channels * self.slots
+        self.small_slots = wide * small_images
+        self.small_rows = channels * self.small_slots
         self.piece_rows = 2 * channels * images
         self.br = WIDTH // wide
         self.bh = self.br // 2
@@ -319,26 +323,38 @@
         return result
 
 
-def local_columns(vec, me, sizes, member):
-    channel = lax.broadcasted_iota(jnp.int32, (sizes.rows, WIDTH), 0) // sizes.slots
-    lane = lax.broadcasted_iota(jnp.int32, (sizes.rows, WIDTH), 1)
-    pick = (lane == 2 * (me * sizes.channels + channel) + member).astype(jnp.float32)
-    return lax.dot_general(
-        pick,
-        vec[0:16],
-        (((1,), (1,)), ((), ())),
-        precision=lax.Precision.HIGHEST,
-        preferred_element_type=jnp.float32,
-    )
+def placements(order_big, order_small, sizes):
+    n, m = sizes.slots, sizes.small_slots
+    big = order_big[...] == lax.broadcasted_iota(jnp.int32, (n, n), 0)
+    small = order_small[...] == lax.broadcasted_iota(jnp.int32, (m, m), 0)
+    slot = lax.broadcasted_iota(jnp.int32, (m, n), 0)
+    padded = lax.broadcasted_iota(jnp.int32, (m, n), 1)
+    inside = padded % sizes.images
+    spread_out = (slot == padded // sizes.images * sizes.small_images + inside) & (
+        inside < sizes.small_images
+    )
+    one = lambda v: v.astype(jnp.float32).astype(jnp.bfloat16)
+    return one(big), nn(one(small), one(spread_out)).astype(jnp.bfloat16)
+
+
+def token_lanes(lens):
+    low = lax.broadcasted_iota(jnp.int32, (1, LANES), 1)
+    high = lax.broadcasted_iota(jnp.int32, (1, 128), 1) + 128
+    return (low >= 1) & (low < lens[0]), (high > SPLIT) & (high < SPLIT + lens[1])
 
 
 def front_kernel(
     sizes,
     lens,
-    cells,
-    heads,
+    act_big,
+    act_small,
+    cls_big,
+    cls_small,
+    order_big,
+    order_small,
     vec,
-    table,
+    table_big,
+    table_small,
     perm,
     mh,
     mqkv,
@@ -346,7 +362,8 @@
     mu,
     md,
     tok,
-    wins,
+    wins_big,
+    wins_small,
     wh,
     wqkv,
     wp,
@@ -360,7 +377,8 @@
     got_head,
     pooled,
     received,
-    totals,
+    sum_big,
+    sum_small,
     one_send,
     one_recv,
     two_send,
@@ -376,21 +394,29 @@
     br, bh, bc = sizes.br, sizes.bh, sizes.bc
     greet((("wide", n_w, me_w), ("dp", n_d, me_d)))
     stage_one[...] = jnp.zeros_like(stage_one)
-    sizes.pack_blocks(stage_one, (mh[...], mqkv[...], mp[...], mu[...], md[...]))
+    sizes.pack_blocks(stage_one, (mh[...], mqkv[...], mp[...], mu[...], jnp.transpose(md[...])))
     got_one[me_d] = stage_one[...].astype(bf16)
     one = spread("dp", n_d, me_d, lambda peer: got_one.at[me_d], got_one.at[me_d], one_send, one_recv)
 
-    taps = [local_columns(vec, me_w, sizes, e) for e in range(2)]
+    n_big, n_small = sizes.slots, sizes.small_slots
+    rows_big = act_big[...].reshape(sizes.rows, act_big.shape[2])
+    rows_small = act_small[...].reshape(sizes.small_rows, act_small.shape[2])
 
     def pool(tap):
-        win = nt(cells[...], table[tap * LANES : (tap + 1) * LANES, :])
-        wins[tap] = win.astype(bf16)
-        for e in range(2):
-            part = taps[e][:, tap : tap + 1] * win
-            if tap == 0:
-                totals[e] = part
-            else:
-                totals[e] += part
+        for rows, table, wins, sums, count in (
+            (rows_big, table_big, wins_big, sum_big, n_big),
+            (rows_small, table_small, wins_small, sum_small, n_small),
+        ):
+            win = nt(rows, table[tap])
+            wins[tap] = win.astype(bf16)
+            for c in range(sizes.channels):
+                own = slice(c * count, (c + 1) * count)
+                for e in range(2):
+                    part = vec[tap, 2 * (me_w * sizes.channels + c) + e] * win[own]
+                    if tap == 0:
+                        sums[e, own] = part
+                    else:
+                        sums[e, own] += part
 
     for tap in range(4):
         pool(tap)
@@ -423,21 +449,28 @@
     for tap in range(4, 9):
         pool(tap)
 
-    big_len, small_len = lens
-    lane = lax.broadcasted_iota(jnp.int32, (1, LANES), 1)
-    token = ((lane >= 1) & (lane < big_len)) | ((lane > SPLIT) & (lane < SPLIT + small_len))
+    put_big, put_small = placements(order_big, order_small, sizes)
+    slot_big = jnp.transpose(put_big.astype(jnp.float32)).astype(bf16)
+    slot_small = jnp.transpose(put_small.astype(jnp.float32)).astype(bf16)
+    head_big, head_small = nt(slot_big, cls_big[...]), nt(slot_small, cls_small[...])
+    token_big, token_small = token_lanes(lens)
+    lane = lax.broadcasted_iota(jnp.int32, (1, 128), 1)
     for e in range(2):
-        rest = jnp.zeros((), jnp.float32)
-        if e == 0:
-            rest = jnp.where(
-                lane == 0, heads[:, 0:1], jnp.where(lane == SPLIT, heads[:, 1:2], 0.0)
+        for c in range(sizes.channels):
+            shift = vec[9, 2 * (me_w * sizes.channels + c) + e]
+            big = jnp.where(token_big, sum_big[e, c * n_big : (c + 1) * n_big] + shift, 0.0)
+            small = jnp.where(
+                token_small, sum_small[e, c * n_small : (c + 1) * n_small] + shift, 0.0
             )
-        full = jnp.where(token, totals[e] + taps[e][:, 9:10], rest)
-        for c in range(sizes.channels):
-            for w in range(n_w):
-                at = (c * n_w + w) * sizes.images
-                to = (e * sizes.channels + c) * sizes.images
-                pooled[w, to : to + sizes.images] = full[at : at + sizes.images].astype(bf16)
+            big = nn(slot_big, big.astype(bf16))
+            low, high = big[:, 0:128], big[:, 128:256] + nn(slot_small, small.astype(bf16))
+            if e == 0:
+                low = jnp.where(lane == 0, head_big[:, c : c + 1], low)
+                high = jnp.where(lane == SPLIT - 128, head_small[:, c : c + 1], high)
+            at = (e * sizes.channels + c) * sizes.images
+            for half, value in enumerate((low, high)):
+                value = value.reshape(n_w, sizes.images, 128).astype(bf16)
+                pooled[:, at : at + sizes.images, half * 128 : half * 128 + 128] = value
     act = spread(
         "wide", n_w, me_w, lambda peer: pooled.at[peer], received.at[me_w], act_send, act_recv
     )
@@ -490,6 +523,8 @@
     gvec,
     gub,
     vec,
+    order_big,
+    order_small,
     perm,
     step,
     sh,
@@ -497,20 +532,26 @@
     sp,
     su,
     sd,
-    table_hbm,
-    wins_hbm,
+    tbig_hbm,
+    tsmall_hbm,
+    wbig_hbm,
+    wsmall_hbm,
     binput_hbm,
     bmodel_hbm,
     bqkv_hbm,
     bhidden_hbm,
-    dact,
-    cols,
+    dact_big,
+    dact_small,
+    dcls_big,
+    dcls_small,
     update,
     states,
     vtotal,
     scalars,
-    table,
-    wins,
+    table_big,
+    table_small,
+    wins_big,
+    wins_small,
     binput,
     bmodel,
     bqkv,
@@ -519,8 +560,9 @@
     outgoing,
     returned,
     grads,
-    weighted,
-    tapsum,
+    mixed_big,
+    mixed_small,
+    taps,
     stage_two,
     stage_head,
     rs_send,
@@ -560,8 +602,10 @@
             (bmodel_hbm, bmodel),
             (bhidden_hbm, bhidden),
             (binput_hbm, binput),
-            (table_hbm, table),
-            (wins_hbm, wins),
+            (wbig_hbm, wins_big),
+            (wsmall_hbm, wins_small),
+            (tbig_hbm, table_big),
+            (tsmall_hbm, table_small),
             (bqkv_hbm, bqkv),
         )
     ):
@@ -624,10 +668,14 @@
     mpack[...] = jnp.zeros_like(mpack)
     for half in range(2):
         sizes.pack_blocks(
-            mpack.at[half], (sh[half], sqkv[half], sp[half], su[half], sd[half])
+            mpack.at[half],
+            (sh[:, half, :], sqkv[half], sp[half], su[half], jnp.transpose(sd[half])),
         )
 
-    taps = [local_columns(vec, me_w, sizes, e) for e in range(2)]
+    put_big, put_small = placements(order_big, order_small, sizes)
+    n_big, n_small = sizes.slots, sizes.small_slots
+    token_big, token_small = token_lanes(lens)
+    lane = lax.broadcasted_iota(jnp.int32, (1, 128), 1)
     for load in loads[3:5]:
         load.wait()
     arrived(back)
@@ -638,40 +686,62 @@
                 at = (e * sizes.channels + c) * sizes.images
                 to = (c * n_w + w) * sizes.images
                 grads[e, to : to + sizes.images] = block[at : at + sizes.images]
-    big_len, small_len = lens
-    lane = lax.broadcasted_iota(jnp.int32, (1, LANES), 1)
-    token = ((lane >= 1) & (lane < big_len)) | ((lane > SPLIT) & (lane < SPLIT + small_len))
-    lane_low = lax.broadcasted_iota(jnp.int32, (1, 128), 1)
-    half_rows = sizes.channels * 8
-
-    def collect(product):
-        part = jnp.sum(product.reshape(sizes.channels, sizes.slots // 8, 8, LANES), 1)
-        return jnp.sum(part.reshape(half_rows, LANES), -1, keepdims=True)
-
-    for e in range(2):
-        tapsum[e] = jnp.where(lane_low == 9, collect(jnp.where(token, grads[e], 0.0)), 0.0)
-    for tap in range(9):
-        win = wins[tap].astype(f32)
-        mixed = jnp.zeros((), f32)
+
+    def fold(big, small):
+        value = jnp.sum(big.reshape(n_big // 8, 8, LANES), 0)
+        return value[:, 0:128] + value[:, 128:256] + jnp.sum(small.reshape(n_small // 8, 8, 128), 0)
+
+    heads_big = jnp.zeros((n_big, 128), f32)
+    heads_small = jnp.zeros((n_small, 128), f32)
+    for c in range(sizes.channels):
+        own_big, own_small = slice(c * n_big, (c + 1) * n_big), slice(c * n_small, (c + 1) * n_small)
+        group = slice(c * 8, (c + 1) * 8)
+        pair = []
         for e in range(2):
-            tapsum[e] = jnp.where(lane_low == tap, collect(grads[e] * win), tapsum[e])
-            mixed += taps[e][:, tap : tap + 1] * grads[e]
-        weighted[:, tap * LANES : (tap + 1) * LANES] = mixed.astype(bf16)
-    cols[...] = jnp.where(lane_low == 0, grads[0, :, 0:128], grads[0, :, 128:256])
+            block = grads[e, own_big].astype(bf16)
+            pair.append((nn(put_big, block), nn(put_small, block[:, 128:256])))
+            taps[9, e, group] = fold(
+                jnp.where(token_big, pair[e][0], 0.0), jnp.where(token_small, pair[e][1], 0.0)
+            )
+        heads_big = jnp.where(lane == c, pair[0][0][:, 0:1], heads_big)
+        heads_small = jnp.where(
+            lane == c, pair[0][1][:, SPLIT - 128 : SPLIT - 127], heads_small
+        )
+        for tap in range(9):
+            big, small = wins_big[tap, own_big].astype(f32), wins_small[tap, own_small].astype(f32)
+            for e in range(2):
+                taps[tap, e, group] = fold(pair[e][0] * big, pair[e][1] * small)
+            one, two = (vec[tap, 2 * (me_w * sizes.channels + c) + e] for e in range(2))
+            mixed_big[own_big, tap * LANES : (tap + 1) * LANES] = (
+                one * pair[0][0] + two * pair[1][0]
+            ).astype(bf16)
+            mixed_small[own_small, tap * 128 : (tap + 1) * 128] = (
+                one * pair[0][1] + two * pair[1][1]
+            ).astype(bf16)
+    dcls_big[...] = heads_big
+    dcls_small[...] = heads_small
+    for load in loads[5:7]:
+        load.wait()
 
     @pl.loop(0, sizes.rows // 256)
     def _(chunk):
         at = pl.ds(pl.multiple_of(chunk * 256, 256), 256)
-        dact[at, :] = nn(weighted[at, :], table[...])
+        dact_big[at, :] = nn(mixed_big[at, :], table_big[...])
+
+    dact_small[...] = nn(mixed_small[...], table_small[...])
 
     vpart[...] = jnp.zeros_like(vpart)
+    half_rows = sizes.channels * 8
     own_channel = lax.broadcasted_iota(jnp.int32, (half_rows, WIDTH), 0) // 8
     own_lane = lax.broadcasted_iota(jnp.int32, (half_rows, WIDTH), 1)
     conv = jnp.zeros((128, WIDTH), f32)
     for e in range(2):
         place = (own_lane == 2 * (me_w * sizes.channels + own_channel) + e).astype(f32)
+        part = jnp.zeros((half_rows, 128), f32)
+        for tap in range(10):
+            part = jnp.where(lane == tap, jnp.sum(taps[tap, e], -1, keepdims=True), part)
         conv += lax.dot_general(
-            tapsum[e],
+            part,
             place,
             (((0,), (0,)), ((), ())),
             precision=lax.Precision.HIGHEST,
@@ -684,7 +754,7 @@
     v_wide[me_w] = vpart[...]
     vec_one = scatter("wide", lambda peer: v_wide.at[me_w], v_wide.at[me_w])
 
-    loads[5].wait()
+    loads[7].wait()
     arrived(first)
     rows_two = rs_got[0].astype(f32)
     rows_head = rsh_got[0].astype(f32)
@@ -822,25 +892,54 @@
 
 
 def finish_kernel(
-    sizes, mh, mqkv, mp, mu, md, vec, vmom, update, states, vtotal, scalars, nvec, nvmom, *outs
+    sizes,
+    mh,
+    mqkv,
+    mp,
+    mu,
+    md,
+    vec,
+    vmom,
+    heads_big,
+    heads_small,
+    update,
+    states,
+    vtotal,
+    scalars,
+    dcls_big,
+    dcls_small,
+    norm,
+    nvec,
+    nvmom,
+    *outs,
 ):
-    factor, fix_one, fix_two = (scalars[0:1, j : j + 1] for j in (1, 2, 3))
+    norm[0] = scalars[0, 0]
+    factor, fix_one, fix_two = (scalars[0, j] for j in (1, 2, 3))
+    dcls_big[...] = jnp.transpose(heads_big[...])[0 : sizes.channels]
+    dcls_small[...] = jnp.transpose(heads_small[...])[0 : sizes.channels]
     updates = sizes.unpack_blocks(update[...])
     firsts = sizes.unpack_blocks(states[0])
     seconds = sizes.unpack_blocks(states[1])
     for member, master in enumerate((mh, mqkv, mp, mu, md)):
-        fresh = master[...] - rate_matrix * updates[member]
+        change, first, second = updates[member], firsts[member], seconds[member]
+        if member == 4:
+            change, first, second = (jnp.transpose(v) for v in (change, first, second))
+        fresh = master[...] - rate_matrix * change
         outs[member][...] = fresh
-        outs[5 + member][0] = firsts[member]
-        outs[5 + member][1] = seconds[member]
+        if member == 0:
+            outs[5][:, 0, :] = first
+            outs[5][:, 1, :] = second
+        else:
+            outs[5 + member][0] = first
+            outs[5 + member][1] = second
         outs[10 + member][...] = fresh.astype(jnp.bfloat16)
     scaled = vtotal[0:23] * factor
-    first = beta_one * vmom[0] + (1.0 - beta_one) * scaled
-    second = beta_two * vmom[1] * vmom[1] + (1.0 - beta_two) * scaled * scaled
+    first = beta_one * vmom[:, 0, :] + (1.0 - beta_one) * scaled
+    second = beta_two * vmom[:, 1, :] * vmom[:, 1, :] + (1.0 - beta_two) * scaled * scaled
     direction = first / fix_one / (jnp.sqrt(second / fix_two) + adam_eps)
     nvec[...] = vec[...] * (1.0 - rate_vector * decay_rate) - rate_vector * direction
-    nvmom[0] = first
-    nvmom[1] = jnp.sqrt(second)
+    nvmom[:, 0, :] = first
+    nvmom[:, 1, :] = jnp.sqrt(second)
 
 
 VM = pl.BlockSpec(memory_space=pltpu.VMEM)
@@ -853,12 +952,13 @@
     return [pltpu.SemaphoreType.DMA((n,)) for n in counts]
 
 
-def run_front(sizes, lens, cells, heads, vec, table, perm, masters):
+def run_front(sizes, lens, acts, orders, vec, tables, perm, masters):
     bf16, f32 = jnp.bfloat16, jnp.float32
     w, d = sizes.wide, sizes.dp
     outs = [
         ((sizes.images, WIDTH, LANES), bf16),
         ((9, sizes.rows, LANES), bf16),
+        ((9, sizes.small_rows, 128), bf16),
         ((WIDTH, WIDTH), bf16),
         ((3, WIDTH, WIDTH), bf16),
         ((WIDTH, WIDTH), bf16),
@@ -867,7 +967,7 @@
     ]
     return pl.pallas_call(
         partial(front_kernel, sizes, lens),
-        in_specs=[VM] * 10,
+        in_specs=[VM] * 6 + [SM] + [VM] * 8,
         out_specs=[VM] * len(outs),
         out_shape=[jax.ShapeDtypeStruct(s, t) for s, t in outs],
         scratch_shapes=[
@@ -880,22 +980,25 @@
             pltpu.VMEM((w, sizes.piece_rows, LANES), bf16),
             pltpu.VMEM((w, sizes.piece_rows, LANES), bf16),
             pltpu.VMEM((2, sizes.rows, LANES), f32),
+            pltpu.VMEM((2, sizes.small_rows, 128), f32),
         ]
         + dma_sems(d - 1, d - 1, w - 1, w - 1, w - 1, w - 1, w - 1, w - 1),
         compiler_params=pltpu.CompilerParams(
             collective_id=0, has_side_effects=True, vmem_limit_bytes=LIMIT
         ),
         name="front",
-    )(cells, heads, vec, table, perm, *masters)
-
-
-def run_tail(sizes, lens, grads, vec, perm, step, moments, table, wins, bases):
+    )(*acts, *orders, vec, *tables, perm, *masters)
+
+
+def run_tail(sizes, lens, grads, vec, orders, perm, step, moments, tables, wins, bases):
     bf16, f32 = jnp.bfloat16, jnp.float32
     w, d = sizes.wide, sizes.dp
     pack = (sizes.pair_rows, sizes.block_lanes)
     outs = [
-        ((sizes.rows, CELLS_PAD), f32),
-        ((sizes.rows, 128), f32),
+        ((sizes.rows, tables[0].shape[1]), f32),
+        ((sizes.small_rows, tables[1].shape[1]), f32),
+        ((sizes.slots, 128), f32),
+        ((sizes.small_slots, 128), f32),
         (pack, f32),
         ((2,) + pack, f32),
         ((24, WIDTH), f32),
@@ -906,17 +1009,18 @@
     piece = (w, sizes.piece_rows, LANES)
     return pl.pallas_call(
         partial(tail_kernel, sizes, lens),
-        in_specs=[VM] * 10 + [SM] + [VM] * 5 + [HB] * 6,
+        in_specs=[VM] * 8 + [SM] + [VM] * 3 + [SM] + [VM] * 5 + [HB] * 8,
         out_specs=[VM] * len(outs),
         out_shape=[jax.ShapeDtypeStruct(s, t) for s, t in outs],
-        scratch_shapes=[pltpu.VMEM(a.shape, a.dtype) for a in (table, wins, *bases)]
-        + dma_sems(6)
+        scratch_shapes=[pltpu.VMEM(a.shape, a.dtype) for a in (*tables, *wins, *bases)]
+        + dma_sems(8)
         + [
             pltpu.VMEM(piece, bf16),
             pltpu.VMEM(piece, bf16),
             pltpu.VMEM((2, sizes.rows, LANES), f32),
             pltpu.VMEM((sizes.rows, 9 * LANES), bf16),
-            pltpu.VMEM((2, sizes.channels * 8, 128), f32),
+            pltpu.VMEM((sizes.small_rows, 9 * 128), bf16),
+            pltpu.VMEM((10, 2, sizes.channels * 8, 128), f32),
             pltpu.VMEM(two, f32),
             pltpu.VMEM(head, f32),
             pltpu.VMEM((w,) + two, bf16),
@@ -946,36 +1050,34 @@
             collective_id=1, has_side_effects=True, vmem_limit_bytes=LIMIT
         ),
         name="tail",
-    )(*grads, vec, perm, step, *moments, table, wins, *bases)
-
-
-def run_finish(sizes, masters, vec, vmom, packs):
+    )(*grads, vec, *orders, perm, step, *moments, *tables, *wins, *bases)
+
+
+def run_finish(sizes, masters, vec, vmom, moments, heads, packs):
     f32, bf16 = jnp.float32, jnp.bfloat16
     shapes = [m.shape for m in masters]
-    outs = [(vec.shape, f32), (vmom.shape, f32)]
-    outs += [(s, f32) for s in shapes] + [((2,) + s, f32) for s in shapes]
+    outs = [((sizes.channels, h.shape[0]), f32) for h in heads]
+    outs += [((1,), f32), (vec.shape, f32), (vmom.shape, f32)]
+    outs += [(s, f32) for s in shapes] + [(m.shape, f32) for m in moments]
     outs += [(s, bf16) for s in shapes]
     return pl.pallas_call(
         partial(finish_kernel, sizes),
-        in_specs=[VM] * 11,
-        out_specs=[VM] * len(outs),
+        in_specs=[VM] * 12 + [SM],
+        out_specs=[VM, VM, SM] + [VM] * (len(outs) - 3),
         out_shape=[jax.ShapeDtypeStruct(s, t) for s, t in outs],
         name="finish",
-    )(*masters, vec, vmom, *packs)
-
-
-def pool_table(grids):
-    table = np.zeros((9, LANES, CELLS_PAD), np.float32)
-    base = 0
-    for grid, side, lane in grids:
-        for tap in range(9):
-            for y in range(side):
-                for x in range(side):
-                    sy, sx = 2 * y + tap // 3 - 1, 2 * x + tap % 3 - 1
-                    if 0 <= sy < grid and 0 <= sx < grid:
-                        table[tap, lane + y * side + x, base + sy * grid + sx] = 1.0
-        base += grid * grid
-    return jnp.asarray(table.reshape(9 * LANES, CELLS_PAD), jnp.bfloat16)
+    )(*masters, vec, vmom, *heads, *packs)
+
+
+def pool_table(grid, side, lane, lanes):
+    table = np.zeros((9, lanes, grid * grid), np.float32)
+    for tap in range(9):
+        for y in range(side):
+            for x in range(side):
+                sy, sx = 2 * y + tap // 3 - 1, 2 * x + tap % 3 - 1
+                if 0 <= sy < grid and 0 <= sx < grid:
+                    table[tap, lane + y * side + x, sy * grid + sx] = 1.0
+    return jnp.asarray(table, jnp.bfloat16)
 
 
 def per_device(
@@ -993,79 +1095,62 @@
     vec_moments,
     *rest,
 ):
-    masters, moments, bases, step = rest[0:5], rest[5:10], rest[10:14], rest[14]
+    masters, moments, bases, step = list(rest[0:5]), list(rest[5:10]), rest[10:14], rest[14]
     channels = big_act.shape[1]
     images, small_images = big_cot.shape[0], small_cot.shape[0]
     lens = (big_cot.shape[1], small_cot.shape[1])
     sizes = Sizes(wide_n, dp_n, channels, images, small_images)
-    big_cells, small_cells = big_act.shape[2], small_act.shape[2]
-    grids = tuple(
-        (int(cells**0.5), int((length - 1) ** 0.5), lane)
-        for cells, length, lane in ((big_cells, lens[0], 1), (small_cells, lens[1], SPLIT + 1))
-    )
-    table = pool_table(grids)
+    side = lambda cells: round(cells**0.5)
+    tables = (
+        pool_table(side(big_act.shape[2]), side(lens[0] - 1), 1, LANES),
+        pool_table(side(small_act.shape[2]), side(lens[1] - 1), SPLIT + 1 - 128, 128),
+    )
     perm = row_permutation(channels, images)
-    take = lambda a, i, axis: jnp.take(a, i, axis=axis, mode="clip")
-
-    big_slots = big_order[0]
-    small_slots = jnp.pad(
-        small_order[0].reshape(wide_n, small_images), ((0, 0), (0, images - small_images))
-    ).reshape(-1)
-    cells = jnp.concatenate(
-        [
-            take(big_act, big_slots, 0),
-            take(small_act, small_slots, 0),
-            jnp.zeros(
-                (big_slots.shape[0], channels, CELLS_PAD - big_cells - small_cells), jnp.bfloat16
-            ),
-        ],
-        2,
-    )
-    cells = jnp.swapaxes(cells, 0, 1).reshape(sizes.rows, CELLS_PAD)
-    heads = jnp.stack([take(big_cls, big_slots, 0), take(small_cls, small_slots, 0)], 2)
-    heads = jnp.swapaxes(heads, 0, 1).reshape(sizes.rows, 2).astype(jnp.float32)
-
-    tok, wins, wh, wqkv, wp, wu, wd = run_front(
-        sizes, lens, cells, heads, vec_params, table, perm, masters
-    )
-    hidden = wu.shape[1]
-    block = run_block(
-        tok, big_cot, small_cot, vec_params, vec_params[19:].reshape(1, hidden), wh, wqkv, wp, wu, wd
-    )
-    dact, cols, update, states, vtotal, scalars = run_tail(
-        sizes, lens, block[2:], vec_params, perm, step, moments, table, wins, bases
-    )
-    results = run_finish(
-        sizes, masters, vec_params, vec_moments, (update, states, vtotal, scalars)
-    )
-
-    ids = lambda n: jnp.arange(n, dtype=jnp.int32)
-    big_count, small_count = big_act.shape[0], small_act.shape[0]
-    big_inverse = jnp.sum(
-        jnp.where(big_slots[:, None] == ids(big_count)[None], ids(big_count)[:, None], 0), 0
-    )
-    small_at = ids(small_count) // small_images * images + ids(small_count) % small_images
-    small_inverse = jnp.sum(
-        jnp.where(small_order[0][:, None] == ids(small_count)[None], small_at[:, None], 0), 0
-    )
-    dact = dact.reshape(channels, sizes.slots, CELLS_PAD)
-    cols = cols.reshape(channels, sizes.slots, 128)
-    low = SPLIT - 128
-    big_act_grad = jnp.swapaxes(take(dact[:, :, :big_cells], big_inverse, 1), 0, 1)
-    small_act_grad = jnp.swapaxes(
-        take(dact[:, :, big_cells : big_cells + small_cells], small_inverse, 1), 0, 1
-    )
-    big_cls_grad = jnp.swapaxes(take(cols[:, :, 0], big_inverse, 1), 0, 1)
-    small_cls_grad = jnp.swapaxes(take(cols[:, :, low], small_inverse, 1), 0, 1)
+    flip = lambda a, i, j: jnp.swapaxes(a, i, j)
+    acts = [flip(a, 0, 1) for a in (big_act, small_act, big_cls, small_cls)]
+    orders = (big_order, small_order)
+    masters[4] = flip(masters[4], 0, 1)
+    moments[0], moments[4] = flip(moments[0], 0, 1), flip(moments[4], 1, 2)
+    vec_moments = flip(vec_moments, 0, 1)
+
+    tok, wins_big, wins_small, wh, wqkv, wp, wu, wd = run_front(
+        sizes, lens, acts, orders, vec_params, tables, perm, masters
+    )
+    block = run_block(tok, flip(big_cot, 1, 2), small_cot, vec_params, wh, wqkv, wp, wu, wd)
+    flat = tuple(t.reshape(-1, t.shape[2]) for t in tables)
+    dact_big, dact_small, *packs = run_tail(
+        sizes,
+        lens,
+        block[2:],
+        vec_params,
+        orders,
+        perm,
+        step,
+        moments,
+        flat,
+        (wins_big, wins_small),
+        bases,
+    )
+    results = list(
+        run_finish(sizes, masters, vec_params, vec_moments, moments, packs[0:2], packs[2:])
+    )
+    cls_big, cls_small, norm, new_vec, new_vec_moments = results[0:5]
+    masters, moments, copies = results[5:10], results[10:15], results[15:20]
+    masters[4], copies[4] = flip(masters[4], 0, 1), flip(copies[4], 0, 1)
+    moments[0], moments[4] = flip(moments[0], 0, 1), flip(moments[4], 1, 2)
     return (
-        block[0],
+        flip(block[0], 1, 2),
         block[1],
-        big_act_grad,
-        big_cls_grad,
-        small_act_grad,
-        small_cls_grad,
-        scalars[0, 0:1],
-        *results,
+        flip(dact_big.reshape(channels, sizes.slots, -1), 0, 1),
+        flip(cls_big, 0, 1),
+        flip(dact_small.reshape(channels, sizes.small_slots, -1), 0, 1),
+        flip(cls_small, 0, 1),
+        norm,
+        new_vec,
+        flip(new_vec_moments, 0, 1),
+        *masters,
+        *moments,
+        *copies,
     )
 
 

time: 188 us -> 142 us (0.76)
  local copies, waits for them, and re-layouts: 46.7 us -> 3.98 us
  other arithmetic: 3.05 us -> 0 us
  Pallas kernels: 135 us -> 137 us
    unnamed x44 -> x4, local copies, waits for them, and re-layouts: 25.8 us -> 3.98 us
    gather x8 -> x0, local copies, waits for them, and re-layouts: 13.6 us -> none  [per_device(): take = lambda a, i, axis: jnp.take(a, i, axis=axis, mode='clip')]
    slice x5 -> x0, local copies, waits for them, and re-layouts: 5.27 us -> none  [the longest x1 1.91 us: per_device(): dact[:, :, :big_cells]]
where the time goes in v1:
time: 142 us
  Pallas kernels  137 us (96%)
  local copies, waits for them, and re-layouts  3.98 us (3%)
    pallas_call x1, Pallas kernels, run_tail(): pl.pallas_call(partial(tail_kernel, sizes, lens), in_specs=[VM] * 8 + [SM...  51 us
    pallas_call x1, Pallas kernels, run_block(): pl.pallas_call(partial(block_kernel, (big_n, small_n, big_len, small_len)...  48.4 us
    pallas_call x1, Pallas kernels, run_front(): pl.pallas_call(partial(front_kernel, sizes, lens), in_specs=[VM] * 6 + [S...  35.3 us
    unnamed x4, local copies, waits for them, and re-layouts  3.98 us

profile of v1, /device:TPU:1, one launch (start us, length us, event | category | flops | bytes accessed | tf_op | source)
XLA Modules:
  0.0 142.1 jit_solution(9033049589811415135)
XLA Ops:
  0.7 35.3 %front.1 = (bf16[8,192,256]{2,1,0:T(8,128)(2,1)}, bf16[9,768,256]{2,1,0:T(8,128)(2,1)}, bf16[9,576,128]{2,1,0:T(8,128)(2,1)}, bf16[192,192]{1,0:T(8,128)(2,1)}, ...) custom-call(bf16[12,64,729]{2,1,0:T(8,128)(2,1)} %bitcast.24, ...), custom_call_target="tpu_custom_call" | custom-call | tf_op jit(solution)/shard_map/front/pallas_call | solution.py:968
  36.0 48.4 %block.1 = (f32[8,192,197]{2,1,0:T(8,128)}, f32[6,37,192]{2,1,0:T(8,128)}, bf16[8,192,256]{2,1,0:T(8,128)(2,1)}, f32[192,192]{1,0:T(8,128)}, f32[3,192,192]{2,1,...) custom-call(bf16[8,192,256]{2,1,0:T(8,128)(2,1)} %get-tuple-element., ...), custom_call_target="tpu_custom_call" | custom-call | tf_op jit(solution)/shard_map/block/pallas_call | solution.py:206
  85.0 51.0 %tail.1 = (f32[768,729]{1,0:T(8,128)}, f32[576,121]{1,0:T(8,128)}, f32[64,128]{1,0:T(8,128)}, f32[48,128]{1,0:T(8,128)}, f32[48,384]{1,0:T(8,128)}, /*index=5*/f...) custom-call(bf16[8,192,256]{2,1,0:T(8,128)(2,1)} %get-tuple-element.78.gtok, f32[192,192]{1,0:T(8,128)} %get-tuple-element.79.gh, ...), custom_call_target="tpu_custom_call" | custom-call | tf_op jit(solution)/shard_map/tail/pallas_call | solution.py:1010
  136.0 2.1 %finish.1 = (f32[12,64]{1,0:T(8,128)}, f32[12,48]{1,0:T(8,128)}, f32[1]{0:T(128)}, f32[23,192]{1,0:T(8,128)}, f32[23,2,192]{2,1,0:T(2,128)}, /*index=5*/f32[12,4...) custom-call(f32[12,48]{1,0:T(8,128)} %mh.3, ...), custom_call_target="tpu_custom_call" | custom-call | tf_op jit(solution)/shard_map/finish/pallas_call | solution.py:1063
  138.1 0.0 copy-start
  138.1 3.3 %copy.55 = f32[64,12,729]{2,0,1:T(8,128)} copy(f32[64,12,729]{2,0,1:T(8,128)} %bitcast.23) | data formatting | bytes 4478976
  141.4 0.0 copy-done
  141.4 0.7 copy.56
Async XLA Ops:
  138.1 3.3 %copy-start = (f32[576,121]{1,0:T(8,128)S(1)}, f32[576,121]{1,0:T(8,128)}, u32[]{:S(2)}) copy-start(f32[576,121]{1,0:T(8,128)} %get-tuple-element.96) | copy-start | bytes 836356

commit v2 on v1

v2 whole, which is shorter than its diff:
```python
from functools import partial

import jax
import jax.numpy as jnp
import numpy as np
from jax import lax
from jax.experimental import pallas as pl
from jax.experimental.pallas import tpu as pltpu
from jax.sharding import PartitionSpec as P

HEADS = 4
HD = 48
beta_one = 0.9
beta_two = 0.999
adam_eps = 1e-08
norm_eps = 1e-06
rate_matrix = 0.08
rate_vector = 0.25
decay_rate = 0.05
clip_limit = 1.0
LANES = 256
SPLIT = 208
SCORE_SCALE = float(HD ** (-0.5) * np.log2(np.e))


def nt(a, b):
    return lax.dot_general(a, b, (((1,), (1,)), ((), ())), preferred_element_type=jnp.float32)


def tn(a, b):
    return lax.dot_general(a, b, (((0,), (0,)), ((), ())), preferred_element_type=jnp.float32)


def nn(a, b):
    return jnp.dot(a, b, preferred_element_type=jnp.float32)


def colsum(v):
    return jnp.sum(v, 0, keepdims=True)


def norm_forward(rows, gain, shift):
    centered = rows - jnp.mean(rows, -1, keepdims=True)
    scale = lax.rsqrt(jnp.mean(centered * centered, -1, keepdims=True) + norm_eps)
    hat = centered * scale
    return hat, scale, (hat * gain + shift).astype(jnp.bfloat16)


def norm_backward(grad, hat, scale, gain):
    inner = grad * gain
    mean_a = jnp.mean(inner, -1, keepdims=True)
    mean_b = jnp.mean(inner * hat, -1, keepdims=True)
    return scale * (inner - mean_a - hat * mean_b)


def block_start(big_len, small_len, vec, sums, bias, cot, ubias):
    for ref in sums:
        ref[...] = jnp.zeros_like(ref)
    cot[...] = jnp.zeros_like(cot)
    width = vec.shape[1]
    for j in range(4):
        ubias[:, j * width : (j + 1) * width] = vec[19 + j : 20 + j]
    key_id = lax.broadcasted_iota(jnp.int32, (LANES, LANES), 1)
    query_id = lax.broadcasted_iota(jnp.int32, (LANES, LANES), 0)
    keep_big = (query_id < SPLIT) & (key_id < big_len)
    keep_small = (query_id >= SPLIT) & (key_id >= SPLIT) & (key_id < SPLIT + small_len)
    bias[...] = jnp.where(keep_big | keep_small, 0.0, -1e30)


def block_step(image, raw, counts, bcot, scot, vec, weights, bout, sout, sums, scratch):
    pair, small_n, big_len, small_len = counts
    wh, wqkv, wp, wu, wd = weights
    gh, gqkv, gp, gu, gdt, gvec, gub = sums
    probs, bias, cot, ubias = scratch
    width = vec.shape[1]
    row_id = lax.broadcasted_iota(jnp.int32, (pair * LANES, 1), 0) % LANES
    lane_id = lax.broadcasted_iota(jnp.int32, (1, width), 1)
    for j in range(pair):
        base = j * LANES
        turned = jnp.transpose(bcot[image + j].astype(jnp.float32))
        cot[base : base + big_len] = turned.astype(jnp.bfloat16)
        small = scot[jnp.minimum(image + j, small_n - 1)].astype(jnp.float32)
        small = jnp.where(image + j < small_n, small, 0.0).astype(jnp.bfloat16)
        cot[base + SPLIT : base + SPLIT + small_len] = small
    raw_low = raw.astype(jnp.bfloat16)
    is_head = (row_id == 0) | (row_id == SPLIT)
    rows = jnp.where(is_head, nn(raw_low, wh[...]) + vec[10:11], raw)
    hat_one, scale_one, normed_one = norm_forward(rows, vec[11:12], vec[12:13])
    queries = (nn(normed_one, wqkv[0]) + vec[13:14]).astype(jnp.bfloat16)
    keys_in = nn(normed_one, wqkv[1]).astype(jnp.bfloat16)
    values = (nn(normed_one, wqkv[2]) + vec[14:15]).astype(jnp.bfloat16)
    zero = jnp.zeros((), jnp.bfloat16)
    in_head = [(lane_id >= h * HD) & (lane_id < (h + 1) * HD) for h in range(HEADS)]
    tiles = [slice(j * LANES, (j + 1) * LANES) for j in range(pair)]
    chains = [(j, h) for h in range(HEADS) for j in range(pair)]
    scores = {
        (j, h): nt(jnp.where(in_head[h], queries[tiles[j]], zero), keys_in[tiles[j]])
        for j, h in chains
    }
    low = {}
    for j, h in chains:
        value = scores[j, h] + bias[...]
        weights = jnp.exp2((value - jnp.max(value, -1, keepdims=True)) * SCORE_SCALE)
        probas = weights * (1.0 / jnp.sum(weights, -1, keepdims=True))
        probs[j, h] = probas
        low[j, h] = probas.astype(jnp.bfloat16)
    mixture = [
        nn(
            jnp.concatenate([low[j, h] for h in range(HEADS)], 1),
            jnp.concatenate([jnp.where(in_head[h], values[tiles[j]], zero) for h in range(HEADS)], 0),
        )
        for j in range(pair)
    ]
    mixture = jnp.concatenate(mixture, 0)
    mixture = mixture.astype(jnp.bfloat16)
    middle = rows + nn(mixture, wp[...]) + vec[15:16]
    hat_two, scale_two, normed_two = norm_forward(middle, vec[16:17], vec[17:18])
    pre = nn(normed_two, wu[...]) + ubias[...]
    cdf = 0.5 + 0.5 * lax.erf(pre * 0.7071067811865476)
    slope = cdf + pre * jnp.exp(pre * pre * -0.5) * 0.3989422804014327
    active = (pre * cdf).astype(jnp.bfloat16)
    result = middle + nn(active, wd[...]) + vec[18:19]
    for j in range(pair):
        bout[image + j] = jnp.transpose(result[tiles[j]])[:, :big_len]
        base = j * LANES + SPLIT
        sout[image + j] = result[base : base + small_len]
    cot_low = cot[...]
    cot_rows = cot_low.astype(jnp.float32)
    gdt[...] += tn(cot_low, active)
    gvec[8:9] += colsum(cot_rows)
    grad_pre = (nt(cot_low, wd[...]) * slope).astype(jnp.bfloat16)
    gu[...] += tn(normed_two, grad_pre)
    gub[...] += colsum(grad_pre.astype(jnp.float32))
    grad_two = nt(grad_pre, wu[...])
    gvec[6:7] += colsum(grad_two * hat_two)
    gvec[7:8] += colsum(grad_two)
    grad_mid = norm_backward(grad_two, hat_two, scale_two, vec[16:17]) + cot_rows
    branch = grad_mid.astype(jnp.bfloat16)
    gp[...] += tn(mixture, branch)
    gvec[5:6] += colsum(branch.astype(jnp.float32))
    grad_mix = nt(branch, wp[...]).astype(jnp.bfloat16)
    own = {(j, h): jnp.where(in_head[h], grad_mix[tiles[j]], zero) for j, h in chains}
    grad_probs = {(j, h): nt(own[j, h], values[tiles[j]]) for j, h in chains}
    grad_scores = {}
    for j, h in chains:
        probas = probs[j, h]
        inner = jnp.sum(probas * grad_probs[j, h], -1, keepdims=True)
        grad_scores[j, h] = (probas * (grad_probs[j, h] - inner)).astype(jnp.bfloat16)
    stack = lambda source: [
        jnp.concatenate([jnp.where(in_head[h], source[tile], zero) for h in range(HEADS)], 0)
        for tile in tiles
    ]
    wide_keys, wide_queries = stack(keys_in), stack(queries)
    all_scores = [jnp.concatenate([grad_scores[j, h] for h in range(HEADS)], 1) for j in range(pair)]
    tall_scores = [jnp.concatenate([grad_scores[j, h] for h in range(HEADS)], 0) for j in range(pair)]
    tall_probs = [
        jnp.concatenate([probs[j, h].astype(jnp.bfloat16) for h in range(HEADS)], 0)
        for j in range(pair)
    ]
    tall_own = [jnp.concatenate([own[j, h] for h in range(HEADS)], 0) for j in range(pair)]
    grad_q = jnp.concatenate([nn(all_scores[j], wide_keys[j]) for j in range(pair)], 0)
    grad_k = jnp.concatenate([tn(tall_scores[j], wide_queries[j]) for j in range(pair)], 0)
    grad_v = jnp.concatenate([tn(tall_probs[j], tall_own[j]) for j in range(pair)], 0)
    grad_q = (grad_q * HD ** (-0.5)).astype(jnp.bfloat16)
    grad_k = (grad_k * HD ** (-0.5)).astype(jnp.bfloat16)
    grad_v = grad_v.astype(jnp.bfloat16)
    gqkv[0] += tn(normed_one, grad_q)
    gqkv[1] += tn(normed_one, grad_k)
    gqkv[2] += tn(normed_one, grad_v)
    gvec[3:4] += colsum(grad_q.astype(jnp.float32))
    gvec[4:5] += colsum(grad_v.astype(jnp.float32))
    grad_one = nt(grad_q, wqkv[0]) + nt(grad_k, wqkv[1]) + nt(grad_v, wqkv[2])
    gvec[1:2] += colsum(grad_one * hat_one)
    gvec[2:3] += colsum(grad_one)
    grad_tok = norm_backward(grad_one, hat_one, scale_one, vec[11:12]) + grad_mid
    grad_head = jnp.where(is_head, grad_tok, 0.0).astype(jnp.bfloat16)
    gh[...] += tn(raw_low, grad_head)
    gvec[0:1] += colsum(grad_head.astype(jnp.float32))
    return jnp.where(is_head, nt(grad_head, wh[...]), grad_tok)


def row_permutation(channels, images):
    width = 192
    group = width // (2 * channels * images)
    table = np.zeros((width, width), np.float32)
    for s in range(group):
        for e in range(2):
            for c in range(channels):
                for i in range(images):
                    row = ((s * 2 + e) * channels + c) * images + i
                    table[row, i * (width // images) + s * 2 * channels + 2 * c + e] = 1.0
    return jnp.asarray(table, jnp.bfloat16)
MESH = pl.DeviceIdType.MESH
WIDTH = 192
PAIR = 2


def up_to(value, unit):
    return -(-value // unit) * unit


def links(axis, count, me, src_of, dst, send, recv, base=0):
    copies = []
    for k in range(1, count):
        peer = lax.rem(me + k, count)
        copies.append(
            pltpu.make_async_remote_copy(
                src_ref=src_of(peer),
                dst_ref=dst,
                send_sem=send.at[base + k - 1],
                recv_sem=recv.at[base + k - 1],
                device_id={axis: peer},
                device_id_type=MESH,
            )
        )
    return copies


def begin(copies):
    for copy in copies:
        copy.start()
    return copies


def arrived(copies):
    for copy in copies:
        copy.wait_recv()


def sent(copies):
    for copy in copies:
        copy.wait_send()


def greet(axes):
    barrier = pltpu.get_barrier_semaphore()
    total = 0
    for axis, count, me in axes:
        for k in range(1, count):
            pl.semaphore_signal(
                barrier,
                inc=1,
                device_id={axis: lax.rem(me + k, count)},
                device_id_type=MESH,
            )
        total += count - 1
    pl.semaphore_wait(barrier, total)


class Sizes:
    def __init__(self, wide, dp, channels, images, small_images):
        self.wide, self.dp = wide, dp
        self.channels, self.images, self.small_images = channels, images, small_images
        self.slots = wide * images
        self.rows = channels * self.slots
        self.small_slots = wide * small_images
        self.small_rows = channels * self.small_slots
        self.piece_rows = 2 * channels * images
        self.pairs = images // PAIR
        self.outputs = 2 * channels
        self.br = WIDTH // wide
        self.bh = self.br // 2
        self.bc = WIDTH // dp
        self.pair_rows = up_to(2 * self.br, 16)
        self.block_lanes = up_to(7 * self.bc, 128)
        self.head_rows = up_to(self.bh, 16)

    def block_places(self):
        br, bh, bc = self.br, self.bh, self.bc
        return (
            [(0, 6 * bc, bh, bc)],
            [(br, 0, br, 3 * bc)],
            [(br, 3 * bc, br, bc)],
            [(0, 0, br, 4 * bc)],
            [(0, 4 * bc, br, bc), (0, 5 * bc, br, bc), (br, 4 * bc, br, bc), (br, 5 * bc, br, bc)],
        )

    def pack_blocks(self, ref, blocks):
        for block, places in zip(blocks, self.block_places()):
            at = 0
            for row, lane, rows, lanes in places:
                ref[row : row + rows, lane : lane + lanes] = block[at : at + rows]
                at += rows

    def unpack_blocks(self, packed):
        result = []
        for places in self.block_places():
            parts = [packed[r : r + n, q : q + m] for r, q, n, m in places]
            result.append(parts[0] if len(parts) == 1 else jnp.concatenate(parts, 0))
        return result


def placements(order_big, order_small, sizes):
    n, m = sizes.slots, sizes.small_slots
    big = order_big[...] == lax.broadcasted_iota(jnp.int32, (n, n), 0)
    small = order_small[...] == lax.broadcasted_iota(jnp.int32, (m, m), 0)
    slot = lax.broadcasted_iota(jnp.int32, (m, n), 0)
    padded = lax.broadcasted_iota(jnp.int32, (m, n), 1)
    inside = padded % sizes.images
    spread_out = (slot == padded // sizes.images * sizes.small_images + inside) & (
        inside < sizes.small_images
    )
    one = lambda v: v.astype(jnp.float32).astype(jnp.bfloat16)
    return one(big), nn(one(small), one(spread_out)).astype(jnp.bfloat16)


def token_lanes(lens):
    low = lax.broadcasted_iota(jnp.int32, (1, LANES), 1)
    high = lax.broadcasted_iota(jnp.int32, (1, 128), 1) + 128
    return (low >= 1) & (low < lens[0]), (high > SPLIT) & (high < SPLIT + lens[1])


VM = pl.BlockSpec(memory_space=pltpu.VMEM)
SM = pl.BlockSpec(memory_space=pltpu.SMEM)
HB = pl.BlockSpec(memory_space=pl.ANY)
LIMIT = 62 * 1024 * 1024 + 512 * 1024


def dma_sems(*counts):
    return [pltpu.SemaphoreType.DMA((n,)) for n in counts]


class Names:
    def __init__(self, names, refs):
        self.__dict__.update(zip(names, refs))
        assert len(names) == len(refs), (len(names), len(refs))


IN_NAMES = [
    "act_small",
    "cls_big",
    "cls_small",
    "order_big",
    "order_small",
    "vec_s",
    "vec",
    "step",
    "perm",
    "table_small",
    "mh",
    "mqkv",
    "mp",
    "mu",
    "md",
    "sh",
    "sqkv",
    "sp",
    "su",
    "sd",
    "act_hbm",
    "table_hbm",
    "bcot_hbm",
    "scot_hbm",
    "binput_hbm",
    "bmodel_hbm",
    "bqkv_hbm",
    "bhidden_hbm",
]
OUT_NAMES = [
    "bout_hbm",
    "sout_hbm",
    "dact_hbm",
    "dsmall_hbm",
    "heads_big",
    "heads_small",
    "update",
    "states",
    "vtotal",
    "scalars",
]


def main_kernel(sizes, lens, scratch_names, *refs):
    bf16, f32 = jnp.bfloat16, jnp.float32
    r = Names(IN_NAMES + OUT_NAMES + scratch_names, refs)
    me_w, me_d = lax.axis_index("wide"), lax.axis_index("dp")
    n_w, n_d = sizes.wide, sizes.dp
    br, bh, bc = sizes.br, sizes.bh, sizes.bc
    half_w = n_w // 2
    partner = me_w + 1 - 2 * lax.rem(me_w, 2)
    n_big, n_small = sizes.slots, sizes.small_slots
    big_len, small_len = lens
    channels, images, outputs = sizes.channels, sizes.images, sizes.outputs

    loads = {}
    for at, name in enumerate(("act", "table", "bcot", "scot", "bmodel", "bhidden", "bqkv", "binput")):
        source = r.bhidden_hbm.at[1] if name == "bhidden" else getattr(r, name + "_hbm")
        loads[name] = pltpu.make_async_copy(source, getattr(r, name), r.load_sem.at[at])
        loads[name].start()

    r.stage_one[...] = jnp.zeros_like(r.stage_one)
    sizes.pack_blocks(
        r.stage_one, (r.mh[...], r.mqkv[...], r.mp[...], r.mu[...], jnp.transpose(r.md[...]))
    )
    r.got_all[me_w, me_d] = r.stage_one[...].astype(bf16)
    r.mpack[me_d] = jnp.zeros(r.mpack.shape[1:], f32)
    greet((("wide", n_w, me_w), ("dp", n_d, me_d)))

    def block_copy(row, column, target, send, recv):
        slot = r.got_all.at[row, column]
        return pltpu.make_async_remote_copy(
            src_ref=slot,
            dst_ref=slot,
            send_sem=send,
            recv_sem=recv,
            device_id=target,
            device_id_type=MESH,
        )

    columns = [lax.rem(me_d + n_d - k, n_d) for k in range(n_d)]
    same_core = [lax.rem(me_w + n_w - 2 * j, n_w) for j in range(half_w)]
    one = [
        block_copy(
            me_w, me_d, {"dp": lax.rem(me_d + k, n_d)}, r.one_send.at[k - 1], r.one_recv.at[k - 1]
        )
        for k in range(1, n_d)
    ]
    across = [
        [
            block_copy(
                me_w,
                columns[k],
                {"wide": lax.rem(me_w + 2 * j, n_w)},
                r.across_send.at[(j - 1) * n_d + k],
                r.across_recv.at[(j - 1) * n_d + k],
            )
            for j in range(1, half_w)
        ]
        for k in range(n_d)
    ]
    inside = [
        [
            block_copy(
                same_core[j],
                columns[k],
                {"wide": partner},
                r.inside_send.at[j * n_d + k],
                r.inside_recv.at[j * n_d + k],
            )
            for k in range(n_d)
        ]
        for j in range(half_w)
    ]
    begin(one)
    begin(across[0])
    inside[0][0].start()

    rows_small = r.act_small[...].reshape(sizes.small_rows, r.act_small.shape[2])

    def tap_value(row, c, e):
        return r.vec_s[row, 2 * (me_w * channels + c) + e]

    def pool(tap):
        rows_big = r.act[...].reshape(sizes.rows, r.act.shape[2])
        for rows, table, wins, sums, count in (
            (rows_big, r.table, r.wins_big, r.sum_big, n_big),
            (rows_small, r.table_small, r.wins_small, r.sum_small, n_small),
        ):
            win = nt(rows, table[tap])
            wins[tap] = win.astype(bf16)
            for c in range(channels):
                own = slice(c * count, (c + 1) * count)
                for e in range(2):
                    part = tap_value(tap, c, e) * win[own]
                    if tap == 0:
                        sums[e, own] = part
                    else:
                        sums[e, own] += part

    loads["act"].wait()
    loads["table"].wait()
    for tap in range(4):
        pool(tap)
    for k in range(1, n_d):
        one[k - 1].wait_recv()
        begin(across[k])
        inside[0][k].start()
    for tap in range(4, 9):
        pool(tap)

    put_big, put_small = placements(r.order_big, r.order_small, sizes)
    slot_big = jnp.transpose(put_big.astype(f32)).astype(bf16)
    slot_small = jnp.transpose(put_small.astype(f32)).astype(bf16)
    head_big, head_small = nt(slot_big, r.cls_big[...]), nt(slot_small, r.cls_small[...])
    token_big, token_small = token_lanes(lens)
    lane = lax.broadcasted_iota(jnp.int32, (1, 128), 1)
    for e in range(2):
        for c in range(channels):
            shift = tap_value(9, c, e)
            big = jnp.where(token_big, r.sum_big[e, c * n_big : (c + 1) * n_big] + shift, 0.0)
            small = jnp.where(
                token_small, r.sum_small[e, c * n_small : (c + 1) * n_small] + shift, 0.0
            )
            big = nn(slot_big, big.astype(bf16))
            low, high = big[:, 0:128], big[:, 128:256] + nn(slot_small, small.astype(bf16))
            if e == 0:
                low = jnp.where(lane == 0, head_big[:, c : c + 1], low)
                high = jnp.where(lane == SPLIT - 128, head_small[:, c : c + 1], high)
            at = (e * channels + c) * images
            for half, value in enumerate((low, high)):
                value = value.reshape(n_w, images, 128).astype(bf16)
                r.swap[:, at : at + images, half * 128 : half * 128 + 128] = value
    per_group = WIDTH // sizes.piece_rows
    piece = WIDTH // images
    for group in range(n_w // per_group):
        block = r.swap[group * per_group : (group + 1) * per_group].reshape(WIDTH, LANES)
        moved = tn(r.perm[...], block).astype(bf16).astype(f32)
        for i in range(images):
            for s in range(per_group):
                at, to = i * piece + s * outputs, i % PAIR * outputs
                r.pooled[i // PAIR, group * per_group + s, to : to + outputs] = moved[
                    at : at + outputs
                ].astype(bf16)

    def forward_links(p):
        return links(
            "wide",
            n_w,
            me_w,
            lambda peer: r.pooled.at[p, peer],
            r.received.at[p, me_w],
            r.act_send,
            r.act_recv,
            p * (n_w - 1),
        )

    def backward_links(p):
        return links(
            "wide",
            n_w,
            me_w,
            lambda peer: r.pooled.at[p, peer],
            r.returned.at[p, me_w],
            r.back_send,
            r.back_recv,
            p * (n_w - 1),
        )

    for p in range(sizes.pairs):
        begin(forward_links(p))
        r.received[p, me_w] = r.pooled[p, me_w]

    for half in range(2):
        sizes.pack_blocks(
            r.mpack.at[me_d, half],
            (r.sh[:, half, :], r.sqkv[half], r.sp[half], r.su[half], jnp.transpose(r.sd[half])),
        )
    moments = begin(
        links("dp", n_d, me_d, lambda p: r.mpack.at[me_d], r.mpack.at[me_d], r.mom_send, r.mom_recv)
    )

    def assemble(w, row):
        for d in range(n_d):
            head, qkv, proj, up, down = sizes.unpack_blocks(r.got_all[w, d].astype(f32))
            r.gu[row(br), d * 4 * bc : (d + 1) * 4 * bc] = up
            for part in range(3):
                low, high = d * 3 * bc, (d + 1) * 3 * bc
                a, b = max(low, part * WIDTH), min(high, (part + 1) * WIDTH)
                if a < b:
                    base = part * WIDTH
                    r.gqkv[part, row(br), a - base : b - base] = qkv[:, a - low : b - low]
            r.gp[row(br), d * bc : (d + 1) * bc] = proj
            r.dact[row(4 * br), d * bc : (d + 1) * bc] = down

    def at_row(w):
        return lambda size: pl.ds(pl.multiple_of(w * size, 8), size)

    aligned = br % 8 == 0
    if aligned:
        assemble(me_w, at_row(me_w))
    for j in range(1, half_w):
        for k in range(n_d):
            across[k][j - 1].wait_recv()
            inside[j][k].start()
        if aligned:
            assemble(same_core[j], at_row(same_core[j]))
    for name in ("bmodel", "bhidden", "bqkv", "binput"):
        loads[name].wait()
    for i in range(6):
        r.bmodel_low[i] = r.bmodel[i].astype(bf16)
    r.bhidden_low[1] = r.bhidden[...].astype(bf16)
    second_hidden = pltpu.make_async_copy(r.bhidden_hbm.at[0], r.bhidden, r.load_sem.at[8])
    second_hidden.start()
    r.bqkv_low[...] = r.bqkv[...].astype(bf16)
    r.binput_low[...] = r.binput[...].astype(bf16)
    for j in range(half_w):
        arrived(inside[j])
        if aligned:
            other = lax.rem(partner + n_w - 2 * j, n_w)
            assemble(other, at_row(other))
    for w in range(n_w):
        if not aligned:
            assemble(w, lambda size: slice(w * size, (w + 1) * size))
        row, lane_at, rows, lanes = sizes.block_places()[0][0]
        for d in range(n_d):
            piece = r.got_all[w, d].astype(f32)
            r.gh[w * bh : (w + 1) * bh, d * bc : (d + 1) * bc] = piece[
                row : row + rows, lane_at : lane_at + lanes
            ]
    even = (
        lax.broadcasted_iota(jnp.int32, (WIDTH // 2, WIDTH), 1)
        == 2 * lax.broadcasted_iota(jnp.int32, (WIDTH // 2, WIDTH), 0)
    ).astype(f32).astype(bf16)
    second_hidden.wait()
    r.bhidden_low[0] = r.bhidden[...].astype(bf16)
    r.wh[...] = tn(even, r.gh[0 : WIDTH // 2].astype(bf16)).astype(bf16)
    r.wqkv[...] = r.gqkv[...].astype(bf16)
    r.wp[...] = r.gp[...].astype(bf16)
    r.wu[...] = r.gu[...].astype(bf16)
    r.wd[...] = r.dact[:, 0:WIDTH].astype(bf16)
    sums = (r.gh, r.gqkv, r.gp, r.gu, r.gdt, r.gvec, r.gub)
    block_start(big_len, small_len, r.vec, sums, r.bias, r.cot, r.ubias)
    loads["bcot"].wait()
    loads["scot"].wait()

    def out_copy(p):
        at = pl.ds(p * PAIR, PAIR)
        return pltpu.make_async_copy(r.bout.at[at], r.bout_hbm.at[at], r.out_sem.at[p])

    @pl.loop(0, sizes.pairs)
    def _(p):
        arrived(forward_links(p))
        block = r.received[p].astype(f32)
        raw = [
            jnp.concatenate([block[w, j * outputs : (j + 1) * outputs] for w in range(n_w)], 0)
            for j in range(PAIR)
        ]
        raw = jnp.concatenate([jnp.transpose(v) for v in raw], 0)
        grad = block_step(
            p * PAIR,
            raw,
            (PAIR, sizes.small_images, big_len, small_len),
            r.bcot,
            r.scot,
            r.vec,
            (r.wh, r.wqkv, r.wp, r.wu, r.wd),
            r.bout,
            r.sout,
            sums,
            (r.probs, r.bias, r.cot, r.ubias),
        )
        sent(forward_links(p))
        for j in range(PAIR):
            turned = jnp.transpose(grad[j * LANES : (j + 1) * LANES])
            for w in range(n_w):
                r.pooled[p, w, j * outputs : (j + 1) * outputs] = turned[
                    w * outputs : (w + 1) * outputs
                ].astype(bf16)
        begin(backward_links(p))
        r.returned[p, me_w] = r.pooled[p, me_w]
        out_copy(p).start()

    small_out = pltpu.make_async_copy(
        r.sout.at[pl.ds(0, sizes.small_images)], r.sout_hbm, r.out_sem.at[sizes.pairs]
    )
    small_out.start()

    u_head = tn(r.binput_low[...], nn(even, r.gh[...].astype(bf16)).astype(bf16))
    u_qkv = [tn(r.bmodel_low[1], r.gqkv[part].astype(bf16)) for part in range(3)]
    u_proj = tn(r.bmodel_low[2], r.gp[...].astype(bf16))
    u_up = tn(r.bmodel_low[4], r.gu[...].astype(bf16))
    u_down = jnp.transpose(nn(r.gdt[...].astype(bf16), r.bhidden_low[1]))
    for copies in (*across, *inside):
        sent(copies)
    r.stage_two[...] = jnp.zeros_like(r.stage_two)
    r.stage_head[...] = jnp.zeros_like(r.stage_head)
    for w in range(n_w):
        at = w * br
        r.stage_two[0:br, 0 : 4 * WIDTH] = u_up[at : at + br]
        for part in range(2):
            r.stage_two[0:br, (4 + part) * WIDTH : (5 + part) * WIDTH] = u_qkv[part][at : at + br]
        r.stage_two[br : 2 * br, 0:WIDTH] = u_qkv[2][at : at + br]
        r.stage_two[br : 2 * br, WIDTH : 2 * WIDTH] = u_proj[at : at + br]
        for j in range(4):
            r.stage_two[br : 2 * br, (2 + j) * WIDTH : (3 + j) * WIDTH] = u_down[
                4 * at + j * br : 4 * at + (j + 1) * br
            ]
        r.stage_head[0:bh] = u_head[w * bh : (w + 1) * bh]
        r.rs_send[w] = r.stage_two[...].astype(bf16)
        r.rsh_send[w] = r.stage_head[...].astype(bf16)
    first = begin(
        links("wide", n_w, me_w, lambda p: r.rs_send.at[p], r.rs_got.at[me_w], r.rs_ss, r.rs_rs)
        + links("wide", n_w, me_w, lambda p: r.rsh_send.at[p], r.rsh_got.at[me_w], r.rsh_ss, r.rsh_rs)
    )
    r.rs_got[me_w] = r.rs_send[me_w]
    r.rsh_got[me_w] = r.rsh_send[me_w]

    for p in range(sizes.pairs):
        arrived(backward_links(p))
    for group in range(n_w // per_group):
        parts = [
            r.returned[i // PAIR, group * per_group + s].astype(f32)[
                i % PAIR * outputs : (i % PAIR + 1) * outputs
            ]
            for i in range(images)
            for s in range(per_group)
        ]
        moved = nn(r.perm[...], jnp.concatenate(parts, 0).astype(bf16))
        for s in range(per_group):
            for e in range(2):
                for c in range(channels):
                    at = s * sizes.piece_rows + (e * channels + c) * images
                    to = (c * n_w + group * per_group + s) * images
                    r.sum_big[e, to : to + images] = moved[at : at + images]

    def fold(big, small):
        value = jnp.sum(big.reshape(n_big // 8, 8, LANES), 0)
        return value[:, 0:128] + value[:, 128:256] + jnp.sum(small.reshape(n_small // 8, 8, 128), 0)

    columns_big = jnp.zeros((n_big, 128), f32)
    columns_small = jnp.zeros((n_small, 128), f32)
    put_big, put_small = placements(r.order_big, r.order_small, sizes)
    for c in range(channels):
        own_big, own_small = slice(c * n_big, (c + 1) * n_big), slice(c * n_small, (c + 1) * n_small)
        group = slice(c * 8, (c + 1) * 8)
        pair = []
        for e in range(2):
            block = r.sum_big[e, own_big].astype(bf16)
            pair.append((nn(put_big, block), nn(put_small, block[:, 128:256])))
            r.taps[9, e, group] = fold(
                jnp.where(token_big, pair[e][0], 0.0), jnp.where(token_small, pair[e][1], 0.0)
            )
        columns_big = jnp.where(lane == c, pair[0][0][:, 0:1], columns_big)
        columns_small = jnp.where(lane == c, pair[0][1][:, SPLIT - 128 : SPLIT - 127], columns_small)
        for tap in range(9):
            big, small = r.wins_big[tap, own_big].astype(f32), r.wins_small[tap, own_small].astype(f32)
            for e in range(2):
                r.taps[tap, e, group] = fold(pair[e][0] * big, pair[e][1] * small)
            up, down = (tap_value(tap, c, e) for e in range(2))
            r.wins_big[tap, own_big] = (up * pair[0][0] + down * pair[1][0]).astype(bf16)
            r.wins_small[tap, own_small] = (up * pair[0][1] + down * pair[1][1]).astype(bf16)
    r.heads_big[...] = columns_big
    r.heads_small[...] = columns_small

    r.vpart[...] = jnp.zeros_like(r.vpart)
    half_rows = channels * 8
    own_channel = lax.broadcasted_iota(jnp.int32, (half_rows, WIDTH), 0) // 8
    own_lane = lax.broadcasted_iota(jnp.int32, (half_rows, WIDTH), 1)
    conv = jnp.zeros((128, WIDTH), f32)
    for e in range(2):
        place = (own_lane == 2 * (me_w * channels + own_channel) + e).astype(f32)
        part = jnp.zeros((half_rows, 128), f32)
        for tap in range(10):
            part = jnp.where(lane == tap, jnp.sum(r.taps[tap, e], -1, keepdims=True), part)
        conv += lax.dot_general(
            part,
            place,
            (((0,), (0,)), ((), ())),
            precision=lax.Precision.HIGHEST,
            preferred_element_type=f32,
        )
    r.vpart[0:10] = conv[0:10]
    r.vpart[10:19] = r.gvec[0:9]
    for j in range(4):
        r.vpart[19 + j : 20 + j] = r.gub[:, j * WIDTH : (j + 1) * WIDTH]
    r.v_wide[me_w] = r.vpart[...]
    vec_one = begin(
        links("wide", n_w, me_w, lambda p: r.v_wide.at[me_w], r.v_wide.at[me_w], r.v1_s, r.v1_r)
    )

    arrived(first)
    rows_two = r.rs_got[0].astype(f32)
    rows_head = r.rsh_got[0].astype(f32)
    for w in range(1, n_w):
        rows_two += r.rs_got[w].astype(f32)
        rows_head += r.rsh_got[w].astype(f32)
    rows_two = rows_two.astype(bf16)
    t_up = nn(rows_two[0:br, 0 : 4 * WIDTH], r.bhidden_low[0])
    t_qkv = nn(rows_two[0:br, 4 * WIDTH : 6 * WIDTH], r.bqkv_low[0 : 2 * WIDTH]) + nn(
        rows_two[br : 2 * br, 0:WIDTH], r.bqkv_low[2 * WIDTH :]
    )
    t_proj = nn(rows_two[br : 2 * br, WIDTH : 2 * WIDTH], r.bmodel_low[3])
    t_down = [
        nn(rows_two[br : 2 * br, (2 + j) * WIDTH : (3 + j) * WIDTH], r.bmodel_low[5])
        for j in range(4)
    ]
    t_head = nn(rows_head.astype(bf16), r.bmodel_low[0])
    for d in range(n_d):
        own = slice(d * bc, (d + 1) * bc)
        sizes.pack_blocks(
            r.stage_one,
            (
                t_head[0:bh, own],
                t_qkv[:, 3 * d * bc : 3 * (d + 1) * bc],
                t_proj[:, own],
                t_up[:, 4 * d * bc : 4 * (d + 1) * bc],
                jnp.concatenate([t[:, own] for t in t_down], 0),
            ),
        )
        r.t_send[d] = r.stage_one[...].astype(bf16)
    second = begin(
        links("dp", n_d, me_d, lambda p: r.t_send.at[p], r.t_got.at[me_d], r.t_ss, r.t_rs)
    )
    r.t_got[me_d] = r.t_send[me_d]
    arrived(vec_one)
    vsum = r.v_wide[0]
    for w in range(1, n_w):
        vsum += r.v_wide[w]
    r.v_dp[me_d] = vsum
    vec_two = begin(links("dp", n_d, me_d, lambda p: r.v_dp.at[me_d], r.v_dp.at[me_d], r.v2_s, r.v2_r))

    def act_part(chunk):
        at = pl.ds(chunk * 256, 256)
        table = r.table[...].reshape(9 * LANES, r.table.shape[2])
        mixed = jnp.concatenate([r.wins_big[tap, at, :] for tap in range(9)], 1)
        r.dact[at, :] = nn(mixed, table)
        copy = pltpu.make_async_copy(
            r.dact.at[at], r.dact_hbm.at[at], r.out_sem.at[sizes.pairs + 2 + chunk]
        )
        copy.start()
        return copy

    chunks = list(range(sizes.rows // 256))
    act_out = [act_part(chunk) for chunk in chunks[:1]]
    arrived(second)
    turned = r.t_got[0].astype(f32)
    for d in range(1, n_d):
        turned += r.t_got[d].astype(f32)
    r.full_got[me_d] = turned.astype(bf16)
    third = begin(
        links("dp", n_d, me_d, lambda p: r.full_got.at[me_d], r.full_got.at[me_d], r.d_s, r.d_r)
    )
    act_out += [act_part(chunk) for chunk in chunks[1:2]]
    arrived(vec_two)
    vsum = r.v_dp[0]
    for d in range(1, n_d):
        vsum += r.v_dp[d]
    r.vtotal[...] = vsum

    def total(value):
        return jnp.sum(jnp.sum(value * value, 0, keepdims=True), -1, keepdims=True)

    vec_square = total(vsum)
    count = jnp.full((8, 128), r.step[0], jnp.int32).astype(f32)[0:1, 0:1]
    fix_one = 1.0 - jnp.exp(count * float(np.log(beta_one)))
    fix_two = 1.0 - jnp.exp(count * float(np.log(beta_two)))
    arrived(third)
    squares = jnp.zeros(r.stage_one.shape, f32)
    for d in range(n_d):
        part = r.full_got[d].astype(f32)
        squares += part * part
    square = jnp.sum(jnp.sum(squares, 0, keepdims=True), -1, keepdims=True)
    r.s_wide[me_w] = jnp.broadcast_to(square, (8, 128))
    fourth = begin(
        links("wide", n_w, me_w, lambda p: r.s_wide.at[me_w], r.s_wide.at[me_w], r.s_s, r.s_r)
    )
    act_out += [act_part(chunk) for chunk in chunks[2:]]
    mixed = jnp.concatenate([r.wins_small[tap] for tap in range(9)], 1)
    r.dsmall[...] = nn(mixed, r.table_small[...].reshape(9 * 128, r.table_small.shape[2]))
    act_out.append(pltpu.make_async_copy(r.dsmall, r.dsmall_hbm, r.out_sem.at[sizes.pairs + 1]))
    act_out[-1].start()
    arrived(moments)
    arrived(fourth)
    square = r.s_wide[0][0:1, 0:1]
    for w in range(1, n_w):
        square += r.s_wide[w][0:1, 0:1]
    norm = jnp.sqrt(square + vec_square)
    factor = jnp.minimum(1.0, clip_limit / (norm + 1e-06))
    which = lax.broadcasted_iota(jnp.int32, (8, 128), 1)
    r.scalars[...] = jnp.where(
        which == 0,
        norm,
        jnp.where(which == 1, factor, jnp.where(which == 2, fix_one, fix_two)),
    )

    def adam(gradient, old):
        scaled = gradient * factor
        moment = beta_one * old[0] + (1.0 - beta_one) * scaled
        second_moment = beta_two * old[1] * old[1] + (1.0 - beta_two) * scaled * scaled
        return moment, second_moment

    for d in range(n_d):
        moment, second_moment = adam(r.full_got[d].astype(f32), r.mpack[d])
        direction = moment / fix_one / (jnp.sqrt(second_moment / fix_two) + adam_eps)
        head, qkv, proj, up, down = sizes.unpack_blocks(direction)
        r.row_head[0:bh, d * bc : (d + 1) * bc] = head
        r.row_qkv[:, 3 * d * bc : 3 * (d + 1) * bc] = qkv
        r.row_proj[:, d * bc : (d + 1) * bc] = proj
        r.row_up[:, 4 * d * bc : 4 * (d + 1) * bc] = up
        r.row_down[:, d * bc : (d + 1) * bc] = down

    def right_rows(ref, size, unit=8):
        return ref[pl.ds(pl.multiple_of(me_d * size, unit), size), :].astype(bf16)

    sizes.pack_blocks(
        r.stage_one,
        (
            nt(r.row_head[...].astype(bf16), right_rows(r.bmodel.at[0], bc))[0:bh],
            nt(r.row_qkv[...].astype(bf16), right_rows(r.bqkv, 3 * bc)),
            nt(r.row_proj[...].astype(bf16), right_rows(r.bmodel.at[3], bc)),
            nt(r.row_up[...].astype(bf16), right_rows(r.bhidden_low.at[0], 4 * bc, 16)),
            nt(r.row_down[...].astype(bf16), right_rows(r.bmodel.at[5], bc)),
        ),
    )
    r.y_got[me_w] = r.stage_one[...].astype(bf16)
    fifth = begin(
        links("wide", n_w, me_w, lambda p: r.y_got.at[me_w], r.y_got.at[me_w], r.y_s, r.y_r)
    )
    moment, second_moment = adam(turned, r.mpack[me_d])
    r.states[0] = moment
    r.states[1] = jnp.sqrt(second_moment)

    def left_rows(ref, size, unit=8):
        if size % unit == 0:
            return ref[pl.ds(pl.multiple_of(me_w * size, unit), size), :].astype(bf16)
        own = lax.broadcasted_iota(jnp.int32, (size, ref.shape[0]), 0) + me_w * size
        pick = own == lax.broadcasted_iota(jnp.int32, (size, ref.shape[0]), 1)
        return nn(pick.astype(f32).astype(bf16), ref[...].astype(bf16)).astype(bf16)

    lefts = (
        left_rows(r.binput, bh),
        left_rows(r.bmodel.at[1], br),
        left_rows(r.bmodel.at[2], br),
        left_rows(r.bmodel.at[4], br),
        left_rows(r.bhidden_low.at[1], 4 * br, 16),
    )
    r.update[...] = jnp.zeros_like(r.update)
    arrived(fifth)
    parts = [sizes.unpack_blocks(r.y_got[w].astype(f32)) for w in range(n_w)]
    sizes.pack_blocks(
        r.update,
        [
            nn(lefts[m], jnp.concatenate([part[m] for part in parts], 0).astype(bf16))
            for m in range(5)
        ],
    )
    for p in range(sizes.pairs):
        sent(backward_links(p))
        out_copy(p).wait()
    small_out.wait()
    for copy in act_out:
        copy.wait()
    for copies in (one, moments, first, vec_one, second, vec_two, third, fourth, fifth):
        sent(copies)


def finish_kernel(
    sizes,
    mh,
    mqkv,
    mp,
    mu,
    md,
    vec,
    vmom,
    heads_big,
    heads_small,
    update,
    states,
    vtotal,
    scalars,
    big_from,
    small_from,
    act_from,
    act_small_from,
    big_to,
    small_to,
    act_to,
    act_small_to,
    dcls_big,
    dcls_small,
    norm,
    nvec,
    nvmom,
    *outs,
):
    outs, (hold_big, hold_small, hold_act, hold_act_small, sem) = outs[:-5], outs[-5:]
    moves = []
    for source, hold, target, parts in (
        (act_from, hold_act, act_to, 4),
        (big_from, hold_big, big_to, 4),
        (act_small_from, hold_act_small, act_small_to, 1),
        (small_from, hold_small, small_to, 1),
    ):
        size = source.shape[0] // parts
        for part in range(parts):
            at = pl.ds(part * size, size)
            pair = [(source.at[at], hold.at[at]), (hold.at[at], target.at[at])]
            moves.append(
                [
                    pltpu.make_async_copy(src, dst, sem.at[which, len(moves)])
                    for which, (src, dst) in enumerate(pair)
                ]
            )
    for move in moves:
        move[0].start()
    norm[0] = scalars[0, 0]
    factor, fix_one, fix_two = (scalars[0, j] for j in (1, 2, 3))
    for move in moves:
        move[0].wait()
        move[1].start()
    dcls_big[...] = jnp.transpose(heads_big[...])[0 : sizes.channels]
    dcls_small[...] = jnp.transpose(heads_small[...])[0 : sizes.channels]
    updates = sizes.unpack_blocks(update[...])
    firsts = sizes.unpack_blocks(states[0])
    seconds = sizes.unpack_blocks(states[1])
    for member, master in enumerate((mh, mqkv, mp, mu, md)):
        change, first, second = updates[member], firsts[member], seconds[member]
        if member == 4:
            change, first, second = (jnp.transpose(v) for v in (change, first, second))
        fresh = master[...] - rate_matrix * change
        outs[member][...] = fresh
        if member == 0:
            outs[5][:, 0, :] = first
            outs[5][:, 1, :] = second
        else:
            outs[5 + member][0] = first
            outs[5 + member][1] = second
        outs[10 + member][...] = fresh.astype(jnp.bfloat16)
    scaled = vtotal[0:23] * factor
    first = beta_one * vmom[:, 0, :] + (1.0 - beta_one) * scaled
    second = beta_two * vmom[:, 1, :] * vmom[:, 1, :] + (1.0 - beta_two) * scaled * scaled
    direction = first / fix_one / (jnp.sqrt(second / fix_two) + adam_eps)
    nvec[...] = vec[...] * (1.0 - rate_vector * decay_rate) - rate_vector * direction
    nvmom[:, 0, :] = first
    nvmom[:, 1, :] = jnp.sqrt(second)

    for move in moves:
        move[1].wait()


def run_main(sizes, lens, ins, hbm):
    bf16, f32 = jnp.bfloat16, jnp.float32
    w, d = sizes.wide, sizes.dp
    images, pairs = sizes.images, sizes.pairs
    act, table, bcot, scot, binput, bmodel, bqkv, bhidden = hbm
    table_small = ins[9]
    small_cells = table_small.shape[2]
    hidden = 4 * WIDTH
    pack = (sizes.pair_rows, sizes.block_lanes)
    two = (sizes.pair_rows, 6 * WIDTH)
    head = (sizes.head_rows, WIDTH)
    swap = (pairs, w, PAIR * sizes.outputs, LANES)
    big, small = sizes.rows, sizes.small_rows
    outs = [
        (bcot.shape, f32),
        (scot.shape, f32),
        ((big, act.shape[2]), f32),
        ((small, small_cells), f32),
        ((sizes.slots, 128), f32),
        ((sizes.small_slots, 128), f32),
        (pack, f32),
        ((2,) + pack, f32),
        ((24, WIDTH), f32),
        ((8, 128), f32),
    ]
    scratch = dict(
        act=(act.shape, bf16),
        table=(table.shape, bf16),
        bcot=(bcot.shape, bf16),
        scot=(scot.shape, bf16),
        binput=(binput.shape, f32),
        bmodel=(bmodel.shape, f32),
        bqkv=(bqkv.shape, f32),
        bhidden=(bhidden.shape[1:], f32),
        binput_low=(binput.shape, bf16),
        bmodel_low=(bmodel.shape, bf16),
        bqkv_low=(bqkv.shape, bf16),
        bhidden_low=(bhidden.shape, bf16),
        stage_one=(pack, f32),
        stage_two=(two, f32),
        stage_head=(head, f32),
        got_all=((w, d) + pack, bf16),
        rs_send=((w,) + two, bf16),
        rsh_send=((w,) + head, bf16),
        mpack=((d, 2) + pack, f32),
        wins_big=((9, big, LANES), bf16),
        wins_small=((9, small, 128), bf16),
        sum_big=((2, big, LANES), f32),
        sum_small=((2, small, 128), f32),
        swap=((w, sizes.piece_rows, LANES), bf16),
        pooled=(swap, bf16),
        received=(swap, bf16),
        returned=(swap, bf16),
        wh=((WIDTH, WIDTH), bf16),
        wqkv=((3, WIDTH, WIDTH), bf16),
        wp=((WIDTH, WIDTH), bf16),
        wu=((WIDTH, hidden), bf16),
        wd=((hidden, WIDTH), bf16),
        gh=((WIDTH, WIDTH), f32),
        gqkv=((3, WIDTH, WIDTH), f32),
        gp=((WIDTH, WIDTH), f32),
        gu=((WIDTH, hidden), f32),
        gdt=((WIDTH, hidden), f32),
        gvec=((16, WIDTH), f32),
        gub=((1, hidden), f32),
        probs=((PAIR, HEADS, LANES, LANES), f32),
        bias=((LANES, LANES), f32),
        cot=((PAIR * LANES, WIDTH), bf16),
        ubias=((1, hidden), f32),
        bout=(bcot.shape, f32),
        sout=((images,) + scot.shape[1:], f32),
        rs_got=((w,) + two, bf16),
        rsh_got=((w,) + head, bf16),
        taps=((10, 2, sizes.channels * 8, 128), f32),
        dact=((big, act.shape[2]), f32),
        dsmall=((small, small_cells), f32),
        vpart=((24, WIDTH), f32),
        v_wide=((w, 24, WIDTH), f32),
        v_dp=((d, 24, WIDTH), f32),
        t_send=((d,) + pack, bf16),
        t_got=((d,) + pack, bf16),
        full_got=((d,) + pack, bf16),
        s_wide=((w, 8, 128), f32),
        row_head=((sizes.bh, WIDTH), f32),
        row_qkv=((sizes.br, 3 * WIDTH), f32),
        row_proj=((sizes.br, WIDTH), f32),
        row_up=((sizes.br, hidden), f32),
        row_down=((4 * sizes.br, WIDTH), f32),
        y_got=((w,) + pack, bf16),
    )
    sems = dict(
        load_sem=9,
        out_sem=pairs + 2 + big // 256,
        one_send=d - 1,
        one_recv=d - 1,
        across_send=(w // 2 - 1) * d,
        across_recv=(w // 2 - 1) * d,
        inside_send=w // 2 * d,
        inside_recv=w // 2 * d,
        act_send=pairs * (w - 1),
        act_recv=pairs * (w - 1),
        back_send=pairs * (w - 1),
        back_recv=pairs * (w - 1),
        mom_send=d - 1,
        mom_recv=d - 1,
    )
    for name in ("rs_ss", "rs_rs", "rsh_ss", "rsh_rs", "v1_s", "v1_r", "s_s", "s_r", "y_s", "y_r"):
        sems[name] = w - 1
    for name in ("t_ss", "t_rs", "v2_s", "v2_r", "d_s", "d_r"):
        sems[name] = d - 1
    return pl.pallas_call(
        partial(main_kernel, sizes, lens, list(scratch) + list(sems)),
        in_specs=[VM] * 5 + [SM, VM, SM] + [VM] * 12 + [HB] * 8,
        out_specs=[HB] * 4 + [VM] * 6,
        out_shape=[jax.ShapeDtypeStruct(s, t) for s, t in outs],
        scratch_shapes=[pltpu.VMEM(s, t) for s, t in scratch.values()] + dma_sems(*sems.values()),
        compiler_params=pltpu.CompilerParams(
            collective_id=0, has_side_effects=True, vmem_limit_bytes=LIMIT
        ),
        name="main",
    )(*ins, *hbm)


def run_finish(sizes, masters, vec, vmom, moments, heads, packs, large):
    f32, bf16 = jnp.float32, jnp.bfloat16
    shapes = [m.shape for m in masters]
    outs = [(a.shape, f32) for a in large]
    outs += [((sizes.channels, h.shape[0]), f32) for h in heads]
    outs += [((1,), f32), (vec.shape, f32), (vmom.shape, f32)]
    outs += [(s, f32) for s in shapes] + [(m.shape, f32) for m in moments]
    outs += [(s, bf16) for s in shapes]
    return pl.pallas_call(
        partial(finish_kernel, sizes),
        in_specs=[VM] * 12 + [SM] + [HB] * 4,
        out_specs=[HB] * 4 + [VM, VM, SM] + [VM] * (len(outs) - 7),
        out_shape=[jax.ShapeDtypeStruct(s, t) for s, t in outs],
        scratch_shapes=[pltpu.VMEM(large[i].shape, f32) for i in range(4)]
        + [pltpu.SemaphoreType.DMA((2, 10))],
        compiler_params=pltpu.CompilerParams(vmem_limit_bytes=LIMIT),
        name="finish",
    )(*masters, vec, vmom, *heads, *packs, *large)


def pool_table(grid, side, lane, lanes):
    table = np.zeros((9, lanes, grid * grid), np.float32)
    for tap in range(9):
        for y in range(side):
            for x in range(side):
                sy, sx = 2 * y + tap // 3 - 1, 2 * x + tap % 3 - 1
                if 0 <= sy < grid and 0 <= sx < grid:
                    table[tap, lane + y * side + x, sy * grid + sx] = 1.0
    return jnp.asarray(table, jnp.bfloat16)


def per_device(
    wide_n,
    dp_n,
    big_act,
    big_cls,
    small_act,
    small_cls,
    big_order,
    small_order,
    big_cot,
    small_cot,
    vec_params,
    vec_moments,
    *rest,
):
    masters, moments, bases, step = list(rest[0:5]), list(rest[5:10]), rest[10:14], rest[14]
    channels = big_act.shape[1]
    images, small_images = big_cot.shape[0], small_cot.shape[0]
    lens = (big_cot.shape[1], small_cot.shape[1])
    sizes = Sizes(wide_n, dp_n, channels, images, small_images)
    side = lambda cells: round(cells**0.5)
    tables = (
        pool_table(side(big_act.shape[2]), side(lens[0] - 1), 1, LANES),
        pool_table(side(small_act.shape[2]), side(lens[1] - 1), SPLIT + 1 - 128, 128),
    )
    perm = row_permutation(channels, images)
    flip = lambda a, i, j: jnp.swapaxes(a, i, j)
    acts = [flip(a, 0, 1) for a in (big_act, small_act, big_cls, small_cls)]
    orders = (big_order, small_order)
    masters[4] = flip(masters[4], 0, 1)
    moments[0], moments[4] = flip(moments[0], 0, 1), flip(moments[4], 1, 2)
    vec_moments = flip(vec_moments, 0, 1)

    ins = (*acts[1:], *orders, vec_params, vec_params, step, perm, tables[1], *masters, *moments)
    hbm = (acts[0], tables[0], flip(big_cot, 1, 2), small_cot, *bases)
    *large, heads_big, heads_small, update, states, vtotal, scalars = run_main(
        sizes, lens, ins, hbm
    )
    packs = (update, states, vtotal, scalars)
    results = list(
        run_finish(
            sizes, masters, vec_params, vec_moments, moments, (heads_big, heads_small), packs, large
        )
    )
    big_out, small_out, dact_big, dact_small = results[0:4]
    results = results[4:]
    cls_big, cls_small, norm, new_vec, new_vec_moments = results[0:5]
    masters, moments, copies = results[5:10], results[10:15], results[15:20]
    masters[4], copies[4] = flip(masters[4], 0, 1), flip(copies[4], 0, 1)
    moments[0], moments[4] = flip(moments[0], 0, 1), flip(moments[4], 1, 2)
    return (
        flip(big_out, 1, 2),
        small_out,
        flip(dact_big.reshape(channels, sizes.slots, -1), 0, 1),
        flip(cls_big, 0, 1),
        flip(dact_small.reshape(channels, sizes.small_slots, -1), 0, 1),
        flip(cls_small, 0, 1),
        norm,
        new_vec,
        flip(new_vec_moments, 0, 1),
        *masters,
        *moments,
        *copies,
    )


def solution(mesh):
    split, wide_first, free = P("dp", "wide", None), P("wide", "dp"), P()
    moment = P(None, "wide", "dp")
    both = P(("dp", "wide"), None, None)
    acts = (split, P("dp", "wide"), split, P("dp", "wide"))
    in_specs = (
        acts
        + (P("dp", None), P("dp", None), both, both, free, free)
        + (wide_first,) * 5
        + (moment,) * 5
        + (free,) * 5
    )
    out_specs = (
        (both, both) + acts + (free,) * 3 + (wide_first,) * 5 + (moment,) * 5 + (wide_first,) * 5
    )
    return jax.shard_map(
        partial(per_device, mesh.shape["wide"], mesh.shape["dp"]),
        mesh=mesh,
        in_specs=in_specs,
        out_specs=out_specs,
        check_vma=False,
    )
```

time: 142 us -> 93.2 us (0.66)
  Pallas kernels: 137 us -> 91.5 us
  local copies, waits for them, and re-layouts: 3.98 us -> 0 us
    pallas_call x4 -> x2, Pallas kernels: 137 us -> 91.5 us  [the longest x1 85.8 us: run_main(): pl.pallas_call(partial(main_kernel, sizes, lens, list(scratch) + list(sem...]
    unnamed x4 -> x0, local copies, waits for them, and re-layouts: 3.98 us -> none
where the time goes in v2:
time: 93.2 us; the launch traced here: 93 us
  Pallas kernels  91.5 us (98%)
  between operations  1.5 us (2%)
    pallas_call x1, Pallas kernels, run_main(): pl.pallas_call(partial(main_kernel, sizes, lens, list(scratch) + list(sem...  85.8 us
    pallas_call x1, Pallas kernels, run_finish(): pl.pallas_call(partial(finish_kernel, sizes), in_specs=[VM] * 12 + [SM] +...  5.7 us

profile of v2, /device:TPU:1, one launch (start us, length us, event | category | flops | bytes accessed | tf_op | source)
XLA Modules:
  0.0 93.0 jit_solution(14465020749586304477)
XLA Ops:
  1.3 85.8 %main.1 = (f32[8,192,197]{2,1,0:T(8,128)}, f32[6,37,192]{2,1,0:T(8,128)}, f32[768,729]{1,0:T(8,128)}, f32[576,121]{1,0:T(8,128)}, f32[64,128]{1,0:T(8,128)}, /*i...) custom-call(bf16[12,48,121]{2,1,0:T(8,128)(2,1)} %bitcast.25, ...), custom_call_target="tpu_custom_call" | custom-call | tf_op jit(solution)/shard_map/main/pallas_call | solution.py:1132
  87.1 5.7 %finish.1 = (f32[8,192,197]{2,1,0:T(8,128)}, f32[6,37,192]{2,1,0:T(8,128)}, f32[768,729]{1,0:T(8,128)}, f32[576,121]{1,0:T(8,128)}, f32[12,64]{1,0:T(8,128)}, /*...) custom-call(f32[12,48]{1,0:T(8,128)} %mh.1, ...), custom_call_target="tpu_custom_call" | custom-call | tf_op jit(solution)/shard_map/finish/pallas_call | solution.py:1153

commit v3 on v2

--- a/solution.py
+++ b/solution.py
@@ -258,6 +258,7 @@
         self.piece_rows = 2 * channels * images
         self.pairs = images // PAIR
         self.outputs = 2 * channels
+        self.vec_share = up_to(24, wide) // wide
         self.br = WIDTH // wide
         self.bh = self.br // 2
         self.bc = WIDTH // dp
@@ -678,12 +679,30 @@
         r.stage_head[0:bh] = u_head[w * bh : (w + 1) * bh]
         r.rs_send[w] = r.stage_two[...].astype(bf16)
         r.rsh_send[w] = r.stage_head[...].astype(bf16)
-    first = begin(
-        links("wide", n_w, me_w, lambda p: r.rs_send.at[p], r.rs_got.at[me_w], r.rs_ss, r.rs_rs)
-        + links("wide", n_w, me_w, lambda p: r.rsh_send.at[p], r.rsh_got.at[me_w], r.rsh_ss, r.rsh_rs)
-    )
-    r.rs_got[me_w] = r.rs_send[me_w]
-    r.rsh_got[me_w] = r.rsh_send[me_w]
+    def pair_copy(source, target, send, recv):
+        return pltpu.make_async_remote_copy(
+            src_ref=source,
+            dst_ref=target,
+            send_sem=send,
+            recv_sem=recv,
+            device_id={"wide": partner},
+            device_id_type=MESH,
+        )
+
+    buffers = ((r.rs_send, r.pair_got, r.rs_got), (r.rsh_send, r.pairh_got, r.rsh_got))
+    targets = [lax.rem(me_w + 2 * j, n_w) for j in range(half_w)]
+    pairs = begin(
+        [
+            pair_copy(
+                source.at[lax.rem(partner + 2 * j, n_w)],
+                got.at[j],
+                r.pair_send.at[which * half_w + j],
+                r.pair_recv.at[which * half_w + j],
+            )
+            for which, (source, got, _) in enumerate(buffers)
+            for j in range(half_w)
+        ]
+    )
 
     for p in range(sizes.pairs):
         arrived(backward_links(p))
@@ -702,6 +721,24 @@
                     at = s * sizes.piece_rows + (e * channels + c) * images
                     to = (c * n_w + group * per_group + s) * images
                     r.sum_big[e, to : to + images] = moved[at : at + images]
+
+    arrived(pairs)
+    first = []
+    for j in range(1, half_w):
+        for which, (source, got, final) in enumerate(buffers):
+            source[targets[j]] = (source[targets[j]].astype(f32) + got[j].astype(f32)).astype(bf16)
+            at = which * (half_w - 1) + j - 1
+            first.append(
+                pltpu.make_async_remote_copy(
+                    src_ref=source.at[targets[j]],
+                    dst_ref=final.at[j],
+                    send_sem=r.first_send.at[at],
+                    recv_sem=r.first_recv.at[at],
+                    device_id={"wide": targets[j]},
+                    device_id_type=MESH,
+                )
+            )
+            first[-1].start()
 
     def fold(big, small):
         value = jnp.sum(big.reshape(n_big // 8, 8, LANES), 0)
@@ -753,17 +790,23 @@
     r.vpart[10:19] = r.gvec[0:9]
     for j in range(4):
         r.vpart[19 + j : 20 + j] = r.gub[:, j * WIDTH : (j + 1) * WIDTH]
-    r.v_wide[me_w] = r.vpart[...]
+    r.v_send[...] = jnp.zeros_like(r.v_send)
+    share = sizes.vec_share
+    for w in range(n_w):
+        r.v_send[w, 0:share] = r.vpart[w * share : (w + 1) * share]
     vec_one = begin(
-        links("wide", n_w, me_w, lambda p: r.v_wide.at[me_w], r.v_wide.at[me_w], r.v1_s, r.v1_r)
-    )
+        links("wide", n_w, me_w, lambda p: r.v_send.at[p], r.v_wide.at[me_w], r.v1_s, r.v1_r)
+    )
+    r.v_wide[me_w] = r.v_send[me_w]
 
     arrived(first)
-    rows_two = r.rs_got[0].astype(f32)
-    rows_head = r.rsh_got[0].astype(f32)
-    for w in range(1, n_w):
-        rows_two += r.rs_got[w].astype(f32)
-        rows_head += r.rsh_got[w].astype(f32)
+    sums_two = []
+    for source, got, final in buffers:
+        rows = source[me_w].astype(f32) + got[0].astype(f32)
+        for j in range(1, half_w):
+            rows += final[j].astype(f32)
+        sums_two.append(rows)
+    rows_two, rows_head = sums_two
     rows_two = rows_two.astype(bf16)
     t_up = nn(rows_two[0:br, 0 : 4 * WIDTH], r.bhidden_low[0])
     t_qkv = nn(rows_two[0:br, 4 * WIDTH : 6 * WIDTH], r.bqkv_low[0 : 2 * WIDTH]) + nn(
@@ -820,41 +863,47 @@
     third = begin(
         links("dp", n_d, me_d, lambda p: r.full_got.at[me_d], r.full_got.at[me_d], r.d_s, r.d_r)
     )
-    act_out += [act_part(chunk) for chunk in chunks[1:2]]
+    def total(value):
+        return jnp.sum(jnp.sum(value * value, 0, keepdims=True), -1, keepdims=True)
+
+    square = total(turned)
     arrived(vec_two)
     vsum = r.v_dp[0]
     for d in range(1, n_d):
         vsum += r.v_dp[d]
-    r.vtotal[...] = vsum
-
-    def total(value):
-        return jnp.sum(jnp.sum(value * value, 0, keepdims=True), -1, keepdims=True)
-
-    vec_square = total(vsum)
+    last_row = lax.broadcasted_iota(jnp.int32, (8, WIDTH), 0) == 7
+    r.s_wide[me_w] = jnp.where(last_row, square, vsum)
+    fourth = begin(
+        links("wide", n_w, me_w, lambda p: r.s_wide.at[me_w], r.s_wide.at[me_w], r.s_s, r.s_r)
+    )
+    act_out += [act_part(chunk) for chunk in chunks[1:2]]
     count = jnp.full((8, 128), r.step[0], jnp.int32).astype(f32)[0:1, 0:1]
     fix_one = 1.0 - jnp.exp(count * float(np.log(beta_one)))
     fix_two = 1.0 - jnp.exp(count * float(np.log(beta_two)))
-    arrived(third)
-    squares = jnp.zeros(r.stage_one.shape, f32)
-    for d in range(n_d):
-        part = r.full_got[d].astype(f32)
-        squares += part * part
-    square = jnp.sum(jnp.sum(squares, 0, keepdims=True), -1, keepdims=True)
-    r.s_wide[me_w] = jnp.broadcast_to(square, (8, 128))
-    fourth = begin(
-        links("wide", n_w, me_w, lambda p: r.s_wide.at[me_w], r.s_wide.at[me_w], r.s_s, r.s_r)
-    )
+    arrived(fourth)
+    square = r.s_wide[0][7:8, 0:1]
+    for w in range(1, n_w):
+        square += r.s_wide[w][7:8, 0:1]
+    r.s_dp[me_d] = jnp.broadcast_to(square, (8, 128))
+    fifth = begin(links("dp", n_d, me_d, lambda p: r.s_dp.at[me_d], r.s_dp.at[me_d], r.s2_s, r.s2_r))
+    vec_squares = jnp.zeros((8, WIDTH), f32)
+    for w in range(n_w):
+        part = jnp.where(last_row, 0.0, r.s_wide[w])
+        vec_squares += part * part
+        r.vtotal[w * share : (w + 1) * share] = part[0:share]
+    vec_square = jnp.sum(jnp.sum(vec_squares, 0, keepdims=True), -1, keepdims=True)
     act_out += [act_part(chunk) for chunk in chunks[2:]]
     mixed = jnp.concatenate([r.wins_small[tap] for tap in range(9)], 1)
     r.dsmall[...] = nn(mixed, r.table_small[...].reshape(9 * 128, r.table_small.shape[2]))
     act_out.append(pltpu.make_async_copy(r.dsmall, r.dsmall_hbm, r.out_sem.at[sizes.pairs + 1]))
     act_out[-1].start()
     arrived(moments)
-    arrived(fourth)
-    square = r.s_wide[0][0:1, 0:1]
-    for w in range(1, n_w):
-        square += r.s_wide[w][0:1, 0:1]
-    norm = jnp.sqrt(square + vec_square)
+    arrived(third)
+    arrived(fifth)
+    square = vec_square
+    for d in range(n_d):
+        square += r.s_dp[d][0:1, 0:1]
+    norm = jnp.sqrt(square)
     factor = jnp.minimum(1.0, clip_limit / (norm + 1e-06))
     which = lax.broadcasted_iota(jnp.int32, (8, 128), 1)
     r.scalars[...] = jnp.where(
@@ -893,9 +942,26 @@
         ),
     )
     r.y_got[me_w] = r.stage_one[...].astype(bf16)
-    fifth = begin(
-        links("wide", n_w, me_w, lambda p: r.y_got.at[me_w], r.y_got.at[me_w], r.y_s, r.y_r)
-    )
+    y_across = begin(
+        [
+            pltpu.make_async_remote_copy(
+                src_ref=r.y_got.at[me_w],
+                dst_ref=r.y_got.at[me_w],
+                send_sem=r.ya_send.at[j - 1],
+                recv_sem=r.ya_recv.at[j - 1],
+                device_id={"wide": targets[j]},
+                device_id_type=MESH,
+            )
+            for j in range(1, half_w)
+        ]
+    )
+    y_inside = [
+        pair_copy(
+            r.y_got.at[same_core[j]], r.y_got.at[same_core[j]], r.yi_send.at[j], r.yi_recv.at[j]
+        )
+        for j in range(half_w)
+    ]
+    y_inside[0].start()
     moment, second_moment = adam(turned, r.mpack[me_d])
     r.states[0] = moment
     r.states[1] = jnp.sqrt(second_moment)
@@ -915,7 +981,10 @@
         left_rows(r.bhidden_low.at[1], 4 * br, 16),
     )
     r.update[...] = jnp.zeros_like(r.update)
-    arrived(fifth)
+    for j in range(1, half_w):
+        y_across[j - 1].wait_recv()
+        y_inside[j].start()
+    arrived(y_inside)
     parts = [sizes.unpack_blocks(r.y_got[w].astype(f32)) for w in range(n_w)]
     sizes.pack_blocks(
         r.update,
@@ -930,7 +999,20 @@
     small_out.wait()
     for copy in act_out:
         copy.wait()
-    for copies in (one, moments, first, vec_one, second, vec_two, third, fourth, fifth):
+    for copies in (
+        one,
+        moments,
+        pairs,
+        first,
+        vec_one,
+        second,
+        vec_two,
+        third,
+        fourth,
+        fifth,
+        y_across,
+        y_inside,
+    ):
         sent(copies)
 
 
@@ -1027,6 +1109,7 @@
     table_small = ins[9]
     small_cells = table_small.shape[2]
     hidden = 4 * WIDTH
+    vec_rows = w * sizes.vec_share
     pack = (sizes.pair_rows, sizes.block_lanes)
     two = (sizes.pair_rows, 6 * WIDTH)
     head = (sizes.head_rows, WIDTH)
@@ -1041,7 +1124,7 @@
         ((sizes.small_slots, 128), f32),
         (pack, f32),
         ((2,) + pack, f32),
-        ((24, WIDTH), f32),
+        ((vec_rows, WIDTH), f32),
         ((8, 128), f32),
     ]
     scratch = dict(
@@ -1090,18 +1173,22 @@
         ubias=((1, hidden), f32),
         bout=(bcot.shape, f32),
         sout=((images,) + scot.shape[1:], f32),
-        rs_got=((w,) + two, bf16),
-        rsh_got=((w,) + head, bf16),
+        rs_got=((w // 2,) + two, bf16),
+        pair_got=((w // 2,) + two, bf16),
+        pairh_got=((w // 2,) + head, bf16),
+        rsh_got=((w // 2,) + head, bf16),
         taps=((10, 2, sizes.channels * 8, 128), f32),
         dact=((big, act.shape[2]), f32),
         dsmall=((small, small_cells), f32),
-        vpart=((24, WIDTH), f32),
-        v_wide=((w, 24, WIDTH), f32),
-        v_dp=((d, 24, WIDTH), f32),
+        vpart=((vec_rows, WIDTH), f32),
+        v_send=((w, 8, WIDTH), f32),
+        v_wide=((w, 8, WIDTH), f32),
+        v_dp=((d, 8, WIDTH), f32),
         t_send=((d,) + pack, bf16),
         t_got=((d,) + pack, bf16),
         full_got=((d,) + pack, bf16),
-        s_wide=((w, 8, 128), f32),
+        s_wide=((w, 8, WIDTH), f32),
+        s_dp=((d, 8, 128), f32),
         row_head=((sizes.bh, WIDTH), f32),
         row_qkv=((sizes.br, 3 * WIDTH), f32),
         row_proj=((sizes.br, WIDTH), f32),
@@ -1123,11 +1210,19 @@
         back_send=pairs * (w - 1),
         back_recv=pairs * (w - 1),
         mom_send=d - 1,
+        pair_send=w,
+        pair_recv=w,
+        first_send=w - 2,
+        first_recv=w - 2,
+        ya_send=w // 2 - 1,
+        ya_recv=w // 2 - 1,
+        yi_send=w // 2,
+        yi_recv=w // 2,
         mom_recv=d - 1,
     )
-    for name in ("rs_ss", "rs_rs", "rsh_ss", "rsh_rs", "v1_s", "v1_r", "s_s", "s_r", "y_s", "y_r"):
+    for name in ("v1_s", "v1_r", "s_s", "s_r"):
         sems[name] = w - 1
-    for name in ("t_ss", "t_rs", "v2_s", "v2_r", "d_s", "d_r"):
+    for name in ("t_ss", "t_rs", "v2_s", "v2_r", "d_s", "d_r", "s2_s", "s2_r"):
         sems[name] = d - 1
     return pl.pallas_call(
         partial(main_kernel, sizes, lens, list(scratch) + list(sems)),

time: 93.2 us -> 89.4 us (0.959)
  Pallas kernels: 91.5 us -> 87.7 us
    pallas_call x1, Pallas kernels: 85.8 us -> 82 us  [run_main(): pl.pallas_call(partial(main_kernel, sizes, lens, list(scratch) + list(sem...]
where the time goes in v3:
time: 89.4 us; the launch traced here: 89.2 us
  Pallas kernels  87.7 us (98%)
  between operations  1.5 us (2%)
    pallas_call x1, Pallas kernels, run_main(): pl.pallas_call(partial(main_kernel, sizes, lens, list(scratch) + list(sem...  82 us
    pallas_call x1, Pallas kernels, run_finish(): pl.pallas_call(partial(finish_kernel, sizes), in_specs=[VM] * 12 + [SM] +...  5.7 us

profile of v3, /device:TPU:1, one launch (start us, length us, event | category | flops | bytes accessed | tf_op | source)
XLA Modules:
  0.0 89.2 jit_solution(1044572633398287039)
XLA Ops:
  1.3 82.0 %main.1 = (f32[8,192,197]{2,1,0:T(8,128)}, f32[6,37,192]{2,1,0:T(8,128)}, f32[768,729]{1,0:T(8,128)}, f32[576,121]{1,0:T(8,128)}, f32[64,128]{1,0:T(8,128)}, /*i...) custom-call(bf16[12,48,121]{2,1,0:T(8,128)(2,1)} %bitcast.25, ...), custom_call_target="tpu_custom_call" | custom-call | tf_op jit(solution)/shard_map/main/pallas_call | solution.py:1227
  83.3 5.7 %finish.1 = (f32[8,192,197]{2,1,0:T(8,128)}, f32[6,37,192]{2,1,0:T(8,128)}, f32[768,729]{1,0:T(8,128)}, f32[576,121]{1,0:T(8,128)}, f32[12,64]{1,0:T(8,128)}, /*...) custom-call(f32[12,48]{1,0:T(8,128)} %mh.1, ...), custom_call_target="tpu_custom_call" | custom-call | tf_op jit(solution)/shard_map/finish/pallas_call | solution.py:1248

commit v4 on v3

--- a/solution.py
+++ b/solution.py
@@ -244,7 +244,7 @@
                 device_id_type=MESH,
             )
         total += count - 1
-    pl.semaphore_wait(barrier, total)
+    return lambda: pl.semaphore_wait(barrier, total)
 
 
 class Sizes:
@@ -383,6 +383,7 @@
     big_len, small_len = lens
     channels, images, outputs = sizes.channels, sizes.images, sizes.outputs
 
+    everybody_here = greet((("wide", n_w, me_w), ("dp", n_d, me_d)))
     loads = {}
     for at, name in enumerate(("act", "table", "bcot", "scot", "bmodel", "bhidden", "bqkv", "binput")):
         source = r.bhidden_hbm.at[1] if name == "bhidden" else getattr(r, name + "_hbm")
@@ -395,8 +396,6 @@
     )
     r.got_all[me_w, me_d] = r.stage_one[...].astype(bf16)
     r.mpack[me_d] = jnp.zeros(r.mpack.shape[1:], f32)
-    greet((("wide", n_w, me_w), ("dp", n_d, me_d)))
-
     def block_copy(row, column, target, send, recv):
         slot = r.got_all.at[row, column]
         return pltpu.make_async_remote_copy(
@@ -442,6 +441,7 @@
         ]
         for j in range(half_w)
     ]
+    everybody_here()
     begin(one)
     begin(across[0])
     inside[0][0].start()
@@ -704,6 +704,24 @@
         ]
     )
 
+    arrived(pairs)
+    first = []
+    for j in range(1, half_w):
+        for which, (source, got, final) in enumerate(buffers):
+            source[targets[j]] = (source[targets[j]].astype(f32) + got[j].astype(f32)).astype(bf16)
+            at = which * (half_w - 1) + j - 1
+            first.append(
+                pltpu.make_async_remote_copy(
+                    src_ref=source.at[targets[j]],
+                    dst_ref=final.at[j],
+                    send_sem=r.first_send.at[at],
+                    recv_sem=r.first_recv.at[at],
+                    device_id={"wide": targets[j]},
+                    device_id_type=MESH,
+                )
+            )
+            first[-1].start()
+
     for p in range(sizes.pairs):
         arrived(backward_links(p))
     for group in range(n_w // per_group):
@@ -721,24 +739,6 @@
                     at = s * sizes.piece_rows + (e * channels + c) * images
                     to = (c * n_w + group * per_group + s) * images
                     r.sum_big[e, to : to + images] = moved[at : at + images]
-
-    arrived(pairs)
-    first = []
-    for j in range(1, half_w):
-        for which, (source, got, final) in enumerate(buffers):
-            source[targets[j]] = (source[targets[j]].astype(f32) + got[j].astype(f32)).astype(bf16)
-            at = which * (half_w - 1) + j - 1
-            first.append(
-                pltpu.make_async_remote_copy(
-                    src_ref=source.at[targets[j]],
-                    dst_ref=final.at[j],
-                    send_sem=r.first_send.at[at],
-                    recv_sem=r.first_recv.at[at],
-                    device_id={"wide": targets[j]},
-                    device_id_type=MESH,
-                )
-            )
-            first[-1].start()
 
     def fold(big, small):
         value = jnp.sum(big.reshape(n_big // 8, 8, LANES), 0)
@@ -880,6 +880,7 @@
     count = jnp.full((8, 128), r.step[0], jnp.int32).astype(f32)[0:1, 0:1]
     fix_one = 1.0 - jnp.exp(count * float(np.log(beta_one)))
     fix_two = 1.0 - jnp.exp(count * float(np.log(beta_two)))
+    inverse_one, inverse_two = 1.0 / fix_one, 1.0 / fix_two
     arrived(fourth)
     square = r.s_wide[0][7:8, 0:1]
     for w in range(1, n_w):
@@ -920,7 +921,7 @@
 
     for d in range(n_d):
         moment, second_moment = adam(r.full_got[d].astype(f32), r.mpack[d])
-        direction = moment / fix_one / (jnp.sqrt(second_moment / fix_two) + adam_eps)
+        direction = moment * inverse_one / (jnp.sqrt(second_moment * inverse_two) + adam_eps)
         head, qkv, proj, up, down = sizes.unpack_blocks(direction)
         r.row_head[0:bh, d * bc : (d + 1) * bc] = head
         r.row_qkv[:, 3 * d * bc : 3 * (d + 1) * bc] = qkv
@@ -1049,8 +1050,8 @@
     outs, (hold_big, hold_small, hold_act, hold_act_small, sem) = outs[:-5], outs[-5:]
     moves = []
     for source, hold, target, parts in (
-        (act_from, hold_act, act_to, 4),
-        (big_from, hold_big, big_to, 4),
+        (act_from, hold_act, act_to, 2),
+        (big_from, hold_big, big_to, 2),
         (act_small_from, hold_act_small, act_small_to, 1),
         (small_from, hold_small, small_to, 1),
     ):

time: 89.4 us -> 88.3 us (0.988)
  Pallas kernels: 87.7 us -> 86.6 us
where the time goes in v4:
time: 88.3 us; the launch traced here: 88.1 us
  Pallas kernels  86.6 us (98%)
  between operations  1.5 us (2%)
    pallas_call x1, Pallas kernels, run_main(): pl.pallas_call(partial(main_kernel, sizes, lens, list(scratch) + list(sem...  81.1 us
    pallas_call x1, Pallas kernels, run_finish(): pl.pallas_call(partial(finish_kernel, sizes), in_specs=[VM] * 12 + [SM] +...  5.48 us

profile of v4, /device:TPU:1, one launch (start us, length us, event | category | flops | bytes accessed | tf_op | source)
XLA Modules:
  0.0 88.1 jit_solution(1100309419221970968)
XLA Ops:
  1.3 81.1 %main.1 = (f32[8,192,197]{2,1,0:T(8,128)}, f32[6,37,192]{2,1,0:T(8,128)}, f32[768,729]{1,0:T(8,128)}, f32[576,121]{1,0:T(8,128)}, f32[64,128]{1,0:T(8,128)}, /*i...) custom-call(bf16[12,48,121]{2,1,0:T(8,128)(2,1)} %bitcast.25, ...), custom_call_target="tpu_custom_call" | custom-call | tf_op jit(solution)/shard_map/main/pallas_call | solution.py:1228
  82.4 5.5 %finish.1 = (f32[8,192,197]{2,1,0:T(8,128)}, f32[6,37,192]{2,1,0:T(8,128)}, f32[768,729]{1,0:T(8,128)}, f32[576,121]{1,0:T(8,128)}, f32[12,64]{1,0:T(8,128)}, /*...) custom-call(f32[12,48]{1,0:T(8,128)} %mh.1, ...), custom_call_target="tpu_custom_call" | custom-call | tf_op jit(solution)/shard_map/finish/pallas_call | solution.py:1249
